TPU v7x, 32 devices: a whole 2x2x4 slice. The times are simulated.
32 devices in a mesh: pipe: 2 (over core), ctx: 4 (over y, x), fsdp: 4 (over z).
Axes of the slice: x: 2, y: 2, z: 4, core: 2. Of those that a mesh axis runs over, the one named last changes fastest.
Arguments:
- tokens: bfloat16 [2, 4, 1024, 960], P(None, 'fsdp', 'ctx'), may hold values from -6 to 6
- cotangent: bfloat16 [2, 4, 1024, 960], P(None, 'fsdp', 'ctx'), may hold values from -6 to 6
- doc_ids: int32 [2, 4, 1024], P(None, 'fsdp'), may hold values from 0 to 8, as said below
- w_query: bfloat16 [2, 960, 960], P('pipe', 'fsdp'), may hold values from -0.1875 to 0.1875
- w_keyval: bfloat16 [2, 960, 640], P('pipe', 'fsdp'), may hold values from -0.1875 to 0.1875
- w_out: bfloat16 [2, 960, 960], P('pipe', 'fsdp'), may hold values from -0.75 to 0.75
- w_gateup: bfloat16 [2, 960, 5120], P('pipe', 'fsdp'), may hold values from -0.1875 to 0.1875
- w_down: bfloat16 [2, 2560, 960], P('pipe', 'fsdp'), may hold values from -0.25 to 0.25
- gain_attn: float32 [2, 960], P('pipe'), may hold values from 0.5 to 1.5
- gain_ffn: float32 [2, 960], P('pipe'), may hold values from 0.5 to 1.5
Outputs:
- section_out: bfloat16 [2, 2, 4, 1024, 960], P('pipe', None, 'fsdp', 'ctx')
- section_in_grad: bfloat16 [2, 2, 4, 1024, 960], P('pipe', None, 'fsdp', 'ctx')
- grad_query: float32 [2, 960, 960], P('pipe', ('ctx', 'fsdp'))
- grad_keyval: float32 [2, 960, 640], P('pipe', ('ctx', 'fsdp'))
- grad_out: float32 [2, 960, 960], P('pipe', ('ctx', 'fsdp'))
- grad_gateup: float32 [2, 960, 5120], P('pipe', ('ctx', 'fsdp'))
- grad_down: float32 [2, 2560, 960], P('pipe', ('ctx', 'fsdp'))
- grad_gain_attn: float32 [2, 960], P('pipe')
- grad_gain_ffn: float32 [2, 960], P('pipe')
Inputs may be any that keep to these rules, and one draw needn't show every extreme that they name: doc_ids never falls along a row and is 0 at the first position and 8 at the last; documents have any length from 1 position to most of a row, and their number may differ from row to row. For each of the 4 rows, in one micro-batch drawn from the seed, some document begins within the first 128 positions and ends within the last 128 positions of the row.
All inputs are finite; a program needn't handle non-finite values.
Results may differ from a plain program's by a relative error of at most 0.023.
Values may be sent and summed in bfloat16 or wider, within the bound.
No kernel may reach another device: no remote copies, remote signals or barrier semaphores. Data moves between devices by JAX's collectives and lax.ppermute only.
A program may use at most 256 MiB of HBM per device.

v0:
```python
import functools
import math

import jax
import jax.numpy as jnp
from jax import lax
from jax.experimental import pallas as pl
from jax.experimental.pallas import tpu as pltpu
from jax.sharding import PartitionSpec as P

HEADS = 15
KV_HEADS = 5
HEAD = 64
GROUPS = HEADS // KV_HEADS
EPSILON = 1e-05
NEGATIVE = -1e30
SCALE = 1.0 / math.sqrt(HEAD)
F32 = jnp.float32
BF16 = jnp.bfloat16


def swap_cores(array):
    return lax.ppermute(array, "pipe", [(0, 1), (1, 0)])


def one_way(array, source, target):
    return lax.ppermute(array, "pipe", [(source, target)])


def across(array, axis, mask):
    count = lax.axis_size(axis)
    return lax.ppermute(array, axis, [(i, i ^ mask) for i in range(count)])


def pick(flag, first, second):
    return jnp.where(flag, first, second)


def two_ways(first, second):
    on_first = lax.axis_index("pipe") == 0
    return pick(on_first, first, second), pick(on_first, second, first)


class Order:
    def __init__(self):
        self.last = None

    def hold(self, *arrays):
        if self.last is not None:
            *arrays, _ = lax.optimization_barrier((*arrays, self.last))
        return arrays[0] if len(arrays) == 1 else tuple(arrays)

    def wait(self, array):
        array = self.hold(array)
        self.last = array
        return array

    def waits(self, arrays):
        arrays = self.hold(*arrays)
        self.last = arrays[0]
        return arrays


def first_way(array):
    pairs = [(c, c ^ 1) for c in range(4)] + [(4 + c, 4 + (c ^ 2)) for c in range(4)]
    return lax.ppermute(array, ("pipe", "ctx"), pairs)


def second_way(array):
    pairs = [(c, c ^ 2) for c in range(4)] + [(4 + c, 4 + (c ^ 1)) for c in range(4)]
    return lax.ppermute(array, ("pipe", "ctx"), pairs)


def dot(left, right):
    return jnp.dot(left, right, preferred_element_type=F32)


def dot_back(left, right):
    return lax.dot_general(left, right, (((1,), (1,)), ((), ())), preferred_element_type=F32)


def dot_rows(left, right):
    return lax.dot_general(left, right, (((0,), (0,)), ((), ())), preferred_element_type=F32)


def normalize(values, gain):
    return values * lax.rsqrt(jnp.mean(values * values, axis=-1, keepdims=True) + EPSILON) * gain


def normalize_back(values, gain, grad):
    inverse = lax.rsqrt(jnp.mean(values * values, axis=-1, keepdims=True) + EPSILON)
    unit = values * inverse
    gain_grad = jnp.sum(grad * unit, axis=0)
    scaled = grad * gain
    return inverse * (scaled - unit * jnp.mean(scaled * unit, axis=-1, keepdims=True)), gain_grad


def angle_tables(token_pos):
    half_size = HEAD // 2
    freqs = jnp.exp(jnp.arange(half_size, dtype=F32) * (-2.0 * math.log(100000.0) / HEAD))
    angles = freqs[:, None] * token_pos[None, :]
    cosine, sine = jnp.cos(angles), jnp.sin(angles)
    return jnp.concatenate([cosine, cosine], axis=0), jnp.concatenate([sine, sine], axis=0)


def rotate(values, tables):
    rows, cols = values.shape
    heads = values.reshape(rows // HEAD, HEAD, cols)
    half = HEAD // 2
    turned = jnp.concatenate([-heads[:, half:], heads[:, :half]], axis=1)
    return (heads * tables[0] + turned * tables[1]).reshape(rows, cols)


def rotate_back(values, tables):
    rows, cols = values.shape
    heads = values.reshape(rows // HEAD, HEAD, cols)
    half = HEAD // 2
    scaled = heads * tables[1]
    turned = jnp.concatenate([scaled[:, half:], -scaled[:, :half]], axis=1)
    return (heads * tables[0] + turned).reshape(rows, cols)


def z_masks():
    count = lax.axis_size("fsdp")
    masks = []
    while count > 1:
        count //= 2
        masks.append(count)
    return masks


class Spread:
    def __init__(self, order, own):
        self.order = order
        held = order.hold(own)[None]
        self.rank = [0]
        for mask in z_masks()[:-2]:
            held = jnp.concatenate([held, across(held, "fsdp", mask)], axis=0)
            self.rank = self.rank + [place ^ mask for place in self.rank]
        self.held = held
        self.flights = [across(held, "fsdp", mask) for mask in (1, 2, 3)]
        self.step = 0

    @classmethod
    def behind(cls, order, held):
        self = cls.__new__(cls)
        self.order, self.held, self.flights, self.rank = order, held, [], None
        self.step = 0
        return self

    def slot(self, number):
        return number if self.rank is None else lax.axis_index("fsdp") ^ self.rank[number]

    def collect(self):
        self.flights = [self.order.wait(flight) for flight in self.flights]

    def advance(self):
        self.step += 1
        if self.step == 1:
            self.collect()
            held = [self.held, *self.flights]
            if self.rank is not None:
                self.rank = [place ^ mask for mask in range(4) for place in self.rank]
            held = self.order.hold(jnp.concatenate(held, axis=0))
            self.flight = first_way(held)
            self.side = second_way(held)
            self.parts = [(held, swap_cores(held))]
        elif self.step == 2:
            got = self.order.wait(self.flight)
            side = self.order.wait(self.side)
            self.flight = second_way(got)
            self.parts.append((got, swap_cores(got)))
            self.parts.append((side, swap_cores(side)))
        else:
            got = self.order.wait(self.flight)
            self.parts.append((got, swap_cores(got)))

    def arrays(self):
        return [part[side] for side in range(2) for part in self.parts]


def place_attn(group):
    arrays = group.arrays()
    depth, rows, cols = arrays[0].shape
    zcount = lax.axis_size("fsdp")
    ccount = lax.axis_size("ctx")

    def body(*refs):
        out, sems = refs[8], refs[9]
        core, ctx = lax.axis_index("pipe"), lax.axis_index("ctx")
        copies = []
        for number in range(8):
            half = core if number < 4 else 1 - core
            mask = 0
            if number % 2 == 1:
                mask = mask ^ (1 + half)
            if number % 4 >= 2:
                mask = mask ^ (2 - half)
            col = pl.multiple_of((ctx ^ mask) * cols, cols)
            for slot in range(depth):
                copies.append(
                    pltpu.make_async_copy(
                        refs[number].at[slot],
                        out.at[group.slot(slot), half, :, pl.ds(col, cols)],
                        sems.at[len(copies)],
                    )
                )
        for copy in copies:
            copy.start()
        for copy in copies:
            copy.wait()

    out = pl.pallas_call(
        body,
        out_shape=jax.ShapeDtypeStruct((zcount, 2, rows, ccount * cols), BF16),
        in_specs=[pl.BlockSpec(memory_space=pl.ANY)] * 8,
        out_specs=pl.BlockSpec(memory_space=pltpu.VMEM),
        scratch_shapes=[pltpu.SemaphoreType.DMA((8 * depth,))],
        compiler_params=pltpu.CompilerParams(vmem_limit_bytes=40 * 1024 * 1024),
        cost_estimate=pl.CostEstimate(flops=0, bytes_accessed=0, transcendentals=0),
    )(*arrays)
    return out.reshape(-1, out.shape[-1])


def first_side(half, ctx):
    return pick(half == 0, ctx % 2, ctx // 2)


class Down:
    def __init__(self, order, piece):
        self.order = order
        self.flight = lax.all_gather(order.hold(piece), "fsdp", axis=0, tiled=False)

    def start(self):
        self.near = self.order.wait(self.flight)
        self.flight = first_way(self.near)
        self.near_other = swap_cores(self.near)

    def finish(self):
        far = self.order.wait(self.flight)
        return [self.near, far, self.near_other, swap_cores(far)]


class Ffn:
    def __init__(self, group, down):
        self.group = group
        self.arrays = group.arrays() + down
        self.depth, self.rows, self.cols = self.arrays[0].shape

    def scratch(self, rows):
        return [
            pltpu.VMEM((4, 2, self.depth * self.rows, self.cols), BF16),
            pltpu.VMEM((4, 2, 2, *self.arrays[8].shape[1:]), BF16),
            pltpu.SemaphoreType.DMA((4, 2 * self.depth)),
            pltpu.SemaphoreType.DMA((16,)),
            pltpu.VMEM((rows, self.arrays[8].shape[2]), F32),
        ]

    def start(self, refs, held, down, sems, down_sems):
        core, ctx = lax.axis_index("pipe"), lax.axis_index("ctx")
        blocks, quarters = [], []
        for number in range(4):
            copies = []
            other = 4 + (0, 2, 1, 3)[number]
            for side, half in ((number, core), (other, 1 - core)):
                for slot in range(self.depth):
                    row = pl.multiple_of(self.group.slot(slot) * self.rows, 16)
                    copies.append(
                        pltpu.make_async_copy(
                            refs[side].at[slot],
                            held.at[number, half, pl.ds(row, self.rows), :],
                            sems.at[number, len(copies)],
                        )
                    )
            blocks.append(copies)
            mask = (0, 1 + core, 2 - core, 3)[number]
            quarters.append(ctx ^ mask)
        downs = []
        for side, half in ((8, core), (9, core), (10, 1 - core), (11, 1 - core)):
            near = first_side(half, ctx)
            for zed in range(4):
                downs.append(
                    pltpu.make_async_copy(
                        refs[side].at[zed],
                        down.at[zed, half, near if side % 2 == 0 else 1 - near],
                        down_sems.at[len(downs)],
                    )
                )
        for copy in blocks[0] + downs + blocks[1] + blocks[2] + blocks[3]:
            copy.start()
        return blocks, quarters, downs

    def call(self, body, outs, *args):
        return pl.pallas_call(
            body,
            out_shape=outs,
            in_specs=[pl.BlockSpec(memory_space=pltpu.VMEM)] * len(args)
            + [pl.BlockSpec(memory_space=pl.ANY)] * 12,
            out_specs=[pl.BlockSpec(memory_space=pltpu.VMEM)] * len(outs),
            scratch_shapes=self.scratch(args[0].shape[0]),
            compiler_params=pltpu.CompilerParams(vmem_limit_bytes=48 * 1024 * 1024),
            cost_estimate=pl.CostEstimate(flops=0, bytes_accessed=0, transcendentals=0),
        )(*args, *self.arrays)

    def forward(self, resid, gain):
        rows, width = resid.shape
        cols = self.cols
        ffn = 4 * cols

        def body(r_ref, gain_ref, *refs):
            low_ref, normed_ref, gate_ref, up_ref, hidden_ref = refs[12:17]
            held, down, total = refs[17], refs[18], refs[21]
            blocks, quarters, downs = self.start(refs[:12], *refs[17:21])
            resid = r_ref[...]
            normed = normalize(resid, gain_ref[...]).astype(BF16)
            normed_ref[...] = normed.T
            total[...] = resid
            for number in range(4):
                for copy in blocks[number]:
                    copy.wait()
                gate = dot(normed, held[number, 0])
                up = dot(normed, held[number, 1])
                hidden = (gate / (1.0 + jnp.exp(-gate)) * up).astype(BF16)
                place = pl.ds(pl.multiple_of(quarters[number] * cols, cols), cols)
                gate_ref[:, place] = gate
                up_ref[:, place] = up
                hidden_ref[place, :] = hidden.T
                if number == 0:
                    for copy in downs:
                        copy.wait()
                weights = down[quarters[number]].reshape(cols, width)
                total[...] += dot(hidden, weights)
            low_ref[...] = total[...].astype(BF16)

        return self.call(
            body,
            [
                jax.ShapeDtypeStruct((rows, width), BF16),
                jax.ShapeDtypeStruct((width, rows), BF16),
                jax.ShapeDtypeStruct((rows, ffn), F32),
                jax.ShapeDtypeStruct((rows, ffn), F32),
                jax.ShapeDtypeStruct((ffn, rows), BF16),
            ],
            resid,
            gain[None],
        )

    def backward(self, grad_low, resid, gain, gate, up):
        rows, width = resid.shape
        cols = self.cols
        ffn = 4 * cols

        def body(grad_ref, r_ref, gain_ref, gate_ref, up_ref, *refs):
            out_ref, gain_out, gate_out, up_out, total = *refs[12:16], refs[20]
            held, down = refs[16:18]
            blocks, quarters, downs = self.start(refs[:12], *refs[16:20])
            grad = grad_ref[...]
            for number in range(4):
                place = pl.ds(pl.multiple_of(quarters[number] * cols, cols), cols)
                if number == 0:
                    for copy in downs:
                        copy.wait()
                weights = down[quarters[number]].reshape(cols, width)
                hidden_grad = dot_back(grad, weights)
                gate, up = gate_ref[:, place], up_ref[:, place]
                sig = 1.0 / (1.0 + jnp.exp(-gate))
                gate_grad = (hidden_grad * up * (sig * (1.0 + gate * (1.0 - sig)))).astype(BF16)
                up_grad = (hidden_grad * (gate * sig)).astype(BF16)
                own, other = two_ways(gate_grad, up_grad)
                gate_out[:, place] = own
                up_out[:, place] = other
                for copy in blocks[number]:
                    copy.wait()
                part = dot_back(gate_grad, held[number, 0]) + dot_back(up_grad, held[number, 1])
                if number == 0:
                    total[...] = part
                else:
                    total[...] += part
            resid_part, gain_grad = normalize_back(r_ref[...], gain_ref[...], total[...])
            out_ref[...] = grad.astype(F32) + resid_part
            gain_out[...] = gain_grad[None]

        outs = self.call(
            body,
            [
                jax.ShapeDtypeStruct((rows, width), F32),
                jax.ShapeDtypeStruct((1, width), F32),
                jax.ShapeDtypeStruct((rows, ffn), BF16),
                jax.ShapeDtypeStruct((rows, ffn), BF16),
            ],
            grad_low,
            resid,
            gain[None],
            gate,
            up,
        )
        return outs[0], outs[1][0], outs[2], outs[3]

    def both(self, resid, gain, grad_low):
        rows, width = resid.shape
        cols = self.cols
        ffn = 4 * cols

        def body(r_ref, gain_ref, grad_ref, *refs):
            low_ref, normed_ref, hidden_ref, out_ref, gain_out, own_ref, send_ref = refs[12:19]
            held, down, total = refs[19], refs[20], refs[23]
            blocks, quarters, downs = self.start(refs[:12], *refs[19:23])
            resid = r_ref[...]
            grad = grad_ref[...]
            normed = normalize(resid, gain_ref[...]).astype(BF16)
            normed_ref[...] = normed.T
            total[...] = resid
            normed_grad = jnp.zeros((rows, width), F32)
            for number in range(4):
                for copy in blocks[number]:
                    copy.wait()
                gate = dot(normed, held[number, 0])
                up = dot(normed, held[number, 1])
                sig = 1.0 / (1.0 + jnp.exp(-gate))
                act = gate / (1.0 + jnp.exp(-gate))
                hidden = (act * up).astype(BF16)
                place = pl.ds(pl.multiple_of(quarters[number] * cols, cols), cols)
                hidden_ref[place, :] = hidden.T
                if number == 0:
                    for copy in downs:
                        copy.wait()
                weights = down[quarters[number]].reshape(cols, width)
                total[...] += dot(hidden, weights)
                hidden_grad = dot_back(grad, weights)
                gate_grad = (hidden_grad * up * (sig * (1.0 + gate * (1.0 - sig)))).astype(BF16)
                up_grad = (hidden_grad * act).astype(BF16)
                own_ref[:, place], send_ref[:, place] = two_ways(gate_grad, up_grad)
                part = dot_back(gate_grad, held[number, 0]) + dot_back(up_grad, held[number, 1])
                normed_grad = normed_grad + part
            low_ref[...] = total[...].astype(BF16)
            resid_part, gain_grad = normalize_back(r_ref[...], gain_ref[...], normed_grad)
            out_ref[...] = grad.astype(F32) + resid_part
            gain_out[...] = gain_grad[None]

        outs = self.call(
            body,
            [
                jax.ShapeDtypeStruct((rows, width), BF16),
                jax.ShapeDtypeStruct((width, rows), BF16),
                jax.ShapeDtypeStruct((ffn, rows), BF16),
                jax.ShapeDtypeStruct((rows, width), F32),
                jax.ShapeDtypeStruct((1, width), F32),
                jax.ShapeDtypeStruct((rows, ffn), BF16),
                jax.ShapeDtypeStruct((rows, ffn), BF16),
            ],
            resid,
            gain[None],
            grad_low,
        )
        return outs[:3], (outs[3], outs[4][0], outs[5], outs[6])


class WholeFfn:
    def __init__(self, w_gateup, w_down, layer):
        core = lax.axis_index("pipe")
        whole = []
        for array in (w_gateup, w_down):
            mine = lax.all_gather(array, "fsdp", axis=0, tiled=True)
            whole.append(pick(core == layer, mine, swap_cores(mine)))
        self.w_gateup, self.w_down = whole

    def forward(self, resid, gain):
        normed = normalize(resid, gain).astype(BF16)
        gated = dot(normed, self.w_gateup)
        ffn = gated.shape[1] // 2
        gate, up = gated[:, :ffn], gated[:, ffn:]
        hidden = (gate / (1.0 + jnp.exp(-gate)) * up).astype(BF16)
        outputs = (resid + dot(hidden, self.w_down)).astype(BF16)
        return outputs, normed.T, gate, up, hidden.T

    def both(self, resid, gain, grad_low):
        outputs, normed, gate, up, hidden = self.forward(resid, gain)
        return (outputs, normed, hidden), self.backward(grad_low, resid, gain, gate, up)

    def backward(self, grad_low, resid, gain, gate, up):
        ffn = gate.shape[1]
        hidden_grad = dot_back(grad_low, self.w_down)
        sig = 1.0 / (1.0 + jnp.exp(-gate))
        gate_grad = (hidden_grad * up * (sig * (1.0 + gate * (1.0 - sig)))).astype(BF16)
        up_grad = (hidden_grad * (gate * sig)).astype(BF16)
        normed_grad = dot_back(gate_grad, self.w_gateup[:, :ffn]) + dot_back(
            up_grad, self.w_gateup[:, ffn:]
        )
        resid_part, gain_grad = normalize_back(resid, gain, normed_grad)
        own, other = two_ways(gate_grad, up_grad)
        return grad_low.astype(F32) + resid_part, gain_grad, own, other


def own_pieces(w_query, w_keyval, w_out, w_gateup, w_down, core, ctx):
    sources = (w_keyval, w_query, w_out)
    rows = w_query.shape[0] // 2
    cols = sum(source.shape[1] for source in sources) // 4
    ffn = w_gateup.shape[1] // 2
    depth = w_down.shape[0] // 2

    def quarter(number):
        found, place = [], 0
        for source in sources:
            start = max(number * cols - place, 0)
            stop = min((number + 1) * cols - place, source.shape[1])
            if start < stop:
                found.append(source[:, start:stop])
            place += source.shape[1]
        return found[0] if len(found) == 1 else jnp.concatenate(found, axis=1)

    attn = pick(
        ctx < 2, pick(ctx == 0, quarter(0), quarter(1)), pick(ctx == 2, quarter(2), quarter(3))
    )
    attn_parts = two_ways(attn[:rows], attn[rows:])

    def parts(half, attn_part):
        return (
            attn_part,
            lax.dynamic_slice(w_gateup, (0, half * ffn + ctx * cols), (2 * rows, cols)),
            lax.dynamic_slice_in_dim(
                w_down, half * depth + first_side(half, ctx) * (depth // 2), depth // 2, 0
            ),
        )

    kept = parts(core, attn_parts[0])
    received = [swap_cores(piece) for piece in parts(1 - core, attn_parts[1])]
    first = [pick(core == 0, a, b) for a, b in zip(kept, received)]
    second = [pick(core == 0, b, a) for a, b in zip(kept, received)]
    return first, second


def add_low(kept, received):
    return (kept.astype(F32) + received.astype(F32)).astype(BF16)


def term(*pairs, gains=None):
    rows = pairs[0][0].shape[0]
    deep = rows // 4
    widths = [pair[2].shape[1] if pair[4] else pair[2].shape[0] for pair in pairs]

    def body(*refs):
        sent_ref, kept_ref = refs[-2:]
        core, ctx = lax.axis_index("pipe"), lax.axis_index("ctx")
        y, x = ctx // 2, ctx % 2
        for out, xx, yy in ((sent_ref, 1 - x, 1 - y), (kept_ref, x, y)):
            for side in range(2):
                block = jnp.where(core == 0, xx + 2 * side, 2 * yy + side)
                place = pl.ds(pl.multiple_of(block * deep, 16), deep)
                offset = 0
                for number, pair in enumerate(pairs):
                    lefts = [ref[place, :] for ref in refs[4 * number : 4 * number + 2]]
                    rights = refs[4 * number + 2 : 4 * number + 4]
                    for start in range(0, widths[number], 640):
                        stop = min(start + 640, widths[number])
                        total = None
                        for left, right in zip(lefts, rights):
                            if pair[4]:
                                part = dot(left, right[:, start:stop])
                            else:
                                part = dot_back(left, right[start:stop, :])
                            total = part if total is None else total + part
                        out[side, :deep, offset + start : offset + stop] = total.astype(BF16)
                    offset += widths[number]
                if gains is not None:
                    out[side, deep:, :] = refs[-3][...]

    extra = []
    if gains is not None:
        low = gains.astype(BF16)
        extra = [jnp.pad(low, ((0, 16 - low.shape[0]), (0, sum(widths) - low.shape[1])))]
    shape = jax.ShapeDtypeStruct((2, deep + 16 * len(extra), sum(widths)), BF16)
    arrays = [array for pair in pairs for array in pair[:4]]
    return local_call(body, [shape, shape], *arrays, *extra)


class Reduce:
    def __init__(self, order, term, offload=False, extra=0):
        self.order = order
        self.extra = extra
        self.offload = offload
        core, ctx, self.zed = lax.axis_index("pipe"), lax.axis_index("ctx"), lax.axis_index("fsdp")
        self.side = pick(core == 0, ctx // 2, ctx % 2)
        self.step = 0
        self.result = None
        sent, kept = term
        self.kept = [kept]
        self.flights = [first_way(sent)]

    def land(self):
        parts = self.kept + [self.order.wait(flight) for flight in self.flights]
        return sum(part.astype(F32) for part in parts)

    def advance(self):
        if self.result is not None:
            return
        index = lax.dynamic_index_in_dim
        self.step += 1
        if self.step == 1:
            parts = self.kept + [self.order.wait(flight) for flight in self.flights]
            sent = sum(index(part, 1 - self.side, 0, False).astype(F32) for part in parts)
            self.kept = [index(part, self.side, 0, False) for part in parts]
            self.flights = [second_way(self.order.wait(sent.astype(BF16)))]
            return
        total = self.land()
        if self.step == 3:
            self.result = total
            return
        low = total.astype(BF16)
        if self.offload:
            count = lax.axis_size("fsdp")
            parts = low.reshape(count, low.shape[0] // count, low.shape[1])
            parts = self.order.wait(parts)
            self.result = lax.psum_scatter(parts, "fsdp", scatter_dimension=0, tiled=False)
            return
        deep = low.shape[0] - self.extra
        body, tail = low[:deep], low[deep:]
        for mask in z_masks()[:-2]:
            half = body.shape[0] // 2
            high = (self.zed & mask) != 0
            self.kept = [jnp.concatenate([pick(high, body[half:], body[:half]), tail], axis=0)]
            sent = jnp.concatenate([pick(high, body[:half], body[half:]), tail], axis=0)
            self.flights = [across(sent, "fsdp", mask)]
            low = self.land().astype(BF16)
            body, tail = low[:half], low[half:]
        parts = body.reshape(4, body.shape[0] // 4, body.shape[1])
        if self.extra:
            tails = jnp.broadcast_to(tail, (4, *tail.shape))
            parts = jnp.concatenate([parts, tails], axis=1)
        here = self.zed % 4
        self.kept = [index(parts, here, 0, False)]
        sent = [index(parts, here ^ mask, 0, False) for mask in (3, 2, 1)]
        sent = self.order.waits(sent)
        self.flights = [across(block, "fsdp", mask) for block, mask in zip(sent, (3, 2, 1))]

    def settle(self):
        self.result = self.order.wait(self.result)


def send_keys(keyval):
    flows = []
    for mask in (3, 1, 2):
        flows.append(across(keyval, "ctx", mask))
    return flows[1], flows[2], flows[0]


def return_keys(parts):
    return [across(part, "ctx", mask) for part, mask in zip(parts, (1, 2, 3))]


def local_call(kernel, outs, *args):
    return pl.pallas_call(
        kernel,
        out_shape=outs,
        in_specs=[pl.BlockSpec(memory_space=pltpu.VMEM)] * len(args),
        out_specs=[pl.BlockSpec(memory_space=pltpu.VMEM)] * len(outs),
        compiler_params=pltpu.CompilerParams(vmem_limit_bytes=48 * 1024 * 1024),
        cost_estimate=pl.CostEstimate(flops=0, bytes_accessed=0, transcendentals=0),
    )(*args)


def project(inputs_low, w_attn, gain_attn, tables):
    rows, width = inputs_low.shape
    kv_width = (w_attn.shape[1] - 2 * width) // 2

    def body(x_ref, w_ref, gain_ref, cos_ref, sin_ref, normed_ref, q_ref, kv_ref):
        tables = cos_ref[...], sin_ref[...]
        normed = normalize(x_ref[...].astype(F32), gain_ref[...]).astype(BF16)
        normed_ref[...] = normed.T
        projected = dot(normed, w_ref[:, : 2 * kv_width + width]).T
        kv_ref[:kv_width, :] = rotate(projected[:kv_width], tables).astype(BF16)
        kv_ref[kv_width:, :] = projected[kv_width : 2 * kv_width].astype(BF16)
        queries = rotate(projected[2 * kv_width :], tables).astype(BF16)
        q_ref[...] = (queries.astype(F32) * SCALE).astype(BF16)

    return local_call(
        body,
        [
            jax.ShapeDtypeStruct((width, rows), BF16),
            jax.ShapeDtypeStruct((width, rows), BF16),
            jax.ShapeDtypeStruct((2 * kv_width, rows), BF16),
        ],
        inputs_low,
        w_attn,
        gain_attn[None],
        *tables,
    )


def head_rows(ref, head, offset=0):
    return ref[pl.ds(pl.multiple_of(head * HEAD + offset, HEAD), HEAD), :]


def attend_kernel(
    q_ref, p0, p1, p2, p3, bias_ref, x_ref, w_ref, normed_ref, own_ref, send_ref, lse_ref, r_ref, o_ref
):
    pieces = (p0, p1, p2, p3)
    count = q_ref.shape[1]
    kv_width = p0.shape[0] // 2
    ones = jnp.ones((16, count), BF16)

    def group(kv_head, carry):
        keys = [head_rows(p, kv_head).T for p in pieces]
        values = [
            jnp.concatenate([head_rows(p, kv_head, kv_width), ones], axis=0) for p in pieces
        ]
        for member in range(GROUPS):
            head = kv_head * GROUPS + member
            query = head_rows(q_ref, head)
            scores = [
                dot(keys[r], query) + bias_ref[r * count : (r + 1) * count, :] for r in range(4)
            ]
            top = jnp.maximum(
                jnp.maximum(scores[0], scores[1]), jnp.maximum(scores[2], scores[3])
            )
            top = jnp.max(top, axis=0, keepdims=True)
            total = jnp.zeros((HEAD + 16, count), F32)
            for r in range(4):
                total = total + dot(values[r], jnp.exp(scores[r] - top).astype(BF16))
            summed = total[HEAD : HEAD + 1]
            o_ref[pl.ds(pl.multiple_of(head * HEAD, HEAD), HEAD), :] = (
                total[:HEAD] / summed
            ).astype(BF16)
            lse_ref[head] = top + jnp.log(summed)
        return carry

    lax.fori_loop(0, KV_HEADS, group, 0)
    attended = o_ref[...]
    own_ref[...], send_ref[...] = two_ways(normed_ref[...], attended)
    width = attended.shape[0]
    r_ref[...] = x_ref[...].astype(F32) + dot(
        attended.T, w_ref[:, w_ref.shape[1] - width :]
    )


def scores_back_kernel(
    dr_ref,
    w_ref,
    q_ref,
    p0,
    p1,
    p2,
    p3,
    bias_ref,
    lse_ref,
    left_own_ref,
    left_send_ref,
    cos_ref,
    sin_ref,
    own_ref,
    send_ref,
    kv_own_ref,
    kv_x_ref,
    kv_y_ref,
    kv_xy_ref,
    do_ref,
    o_ref,
    dq_ref,
):
    tables = cos_ref[...], sin_ref[...]
    width = q_ref.shape[0]
    resid_low = dr_ref[...].astype(BF16)
    do_ref[...] = dot_back(w_ref[:, w_ref.shape[1] - width :], resid_low).astype(BF16)
    _, o_ref[...] = two_ways(left_own_ref[...], left_send_ref[...])
    pieces = (p0, p1, p2, p3)
    count = q_ref.shape[1]
    kv_width = p0.shape[0] // 2

    def group(kv_head, carry):
        keys_turned = [head_rows(p, kv_head) for p in pieces]
        keys = [k.T for k in keys_turned]
        values = [head_rows(p, kv_head, kv_width).T for p in pieces]
        key_grads = [jnp.zeros((HEAD, count), F32) for _ in range(4)]
        value_grads = [jnp.zeros((HEAD, count), F32) for _ in range(4)]
        for member in range(GROUPS):
            head = kv_head * GROUPS + member
            query = head_rows(q_ref, head)
            grad = head_rows(do_ref, head)
            delta = jnp.sum(
                grad.astype(F32) * head_rows(o_ref, head).astype(F32), axis=0, keepdims=True
            )
            log_total = lse_ref[head]
            query_grad = jnp.zeros((HEAD, count), F32)
            for r in range(4):
                scores = dot(keys[r], query) + bias_ref[r * count : (r + 1) * count, :]
                probs = jnp.exp(scores - log_total)
                prob_grad = dot(values[r], grad)
                score_low = (probs * (prob_grad - delta)).astype(BF16)
                value_grads[r] = value_grads[r] + dot_back(grad, probs.astype(BF16))
                key_grads[r] = key_grads[r] + dot_back(query, score_low)
                query_grad = query_grad + dot(keys_turned[r], score_low)
            dq_ref[pl.ds(pl.multiple_of(head * HEAD, HEAD), HEAD), :] = rotate_back(
                query_grad * SCALE, tables
            ).astype(BF16)
        start = pl.multiple_of(kv_head * HEAD, HEAD)
        for r, ref in enumerate((kv_own_ref, kv_x_ref, kv_y_ref, kv_xy_ref)):
            ref[pl.ds(start, HEAD), :] = key_grads[r].astype(ref.dtype)
            place = pl.ds(pl.multiple_of(start + kv_width, HEAD), HEAD)
            ref[place, :] = value_grads[r].astype(ref.dtype)
        return carry

    lax.fori_loop(0, KV_HEADS, group, 0)
    own_ref[...], send_ref[...] = two_ways(dq_ref[...], resid_low.T)


def attend(inputs_low, projected, pieces, w_attn, bias):
    normed, queries, _ = projected
    width, rows = queries.shape
    left_own, left_send, log_total, resid, _ = local_call(
        attend_kernel,
        [
            jax.ShapeDtypeStruct((width, rows), BF16),
            jax.ShapeDtypeStruct((width, rows), BF16),
            jax.ShapeDtypeStruct((HEADS, 1, rows), F32),
            jax.ShapeDtypeStruct((rows, width), F32),
            jax.ShapeDtypeStruct((width, rows), BF16),
        ],
        queries,
        *pieces,
        bias,
        inputs_low,
        w_attn,
        normed,
    )
    lefts = (left_own, swap_cores(left_send), normed, swap_cores(normed))
    return resid, (inputs_low, queries, pieces, log_total, left_own, left_send, lefts)


def backward_scores(resid_grad, saved, w_attn, bias, tables):
    _, queries, pieces, log_total, left_own, left_send, _ = saved
    width, rows = queries.shape
    keys = pieces[0].shape
    return local_call(
        scores_back_kernel,
        [
            jax.ShapeDtypeStruct((width, rows), BF16),
            jax.ShapeDtypeStruct((width, rows), BF16),
            jax.ShapeDtypeStruct(keys, F32),
            jax.ShapeDtypeStruct(keys, BF16),
            jax.ShapeDtypeStruct(keys, BF16),
            jax.ShapeDtypeStruct(keys, BF16),
            jax.ShapeDtypeStruct((width, rows), BF16),
            jax.ShapeDtypeStruct((width, rows), BF16),
            jax.ShapeDtypeStruct((width, rows), BF16),
        ],
        resid_grad,
        w_attn,
        queries,
        *pieces,
        bias,
        log_total,
        left_own,
        left_send,
        *tables,
    )[:6]


def backward_project(resid_grad, rights, kv_own, flows, saved, w_attn, gain_attn, tables):
    inputs_low = saved[0]
    rows, width = inputs_low.shape
    kv_width = kv_own.shape[0] // 2

    def body(
        dr_ref, own, send, kv0, kv1, kv2, kv3, x_ref, w_ref, gain_ref, cos_ref, sin_ref,
        low_ref, gain_out, thin_own, thin_send,
    ):
        tables = cos_ref[...], sin_ref[...]
        kv = kv0[...]
        for ref in (kv1, kv2, kv3):
            kv = kv + ref[...].astype(F32)
        keys = rotate_back(kv[:kv_width], tables).astype(BF16)
        values = kv[kv_width:].astype(BF16)
        queries, _ = two_ways(own[...], send[...])
        thin_own[...], thin_send[...] = two_ways(keys, values)
        projected = jnp.concatenate([keys, values, queries], axis=0).T
        normed_grad = dot_back(projected, w_ref[:, : 2 * kv_width + width])
        part, gain_grad = normalize_back(
            x_ref[...].astype(F32), gain_ref[...], normed_grad
        )
        low_ref[...] = (dr_ref[...] + part).astype(BF16)
        gain_out[...] = gain_grad[None]

    low, gain_grad, thin_own, thin_send = local_call(
        body,
        [
            jax.ShapeDtypeStruct((rows, width), BF16),
            jax.ShapeDtypeStruct((1, width), F32),
            jax.ShapeDtypeStruct((kv_width, rows), BF16),
            jax.ShapeDtypeStruct((kv_width, rows), BF16),
        ],
        resid_grad,
        *rights,
        kv_own,
        *flows,
        inputs_low,
        w_attn,
        gain_attn[None],
        *tables,
    )
    return low, gain_grad[0], thin_own, thin_send


def shards(
    tokens, cotangent, doc_ids, w_query, w_keyval, w_out, w_gateup, w_down, gain_attn, gain_ffn
):
    core = lax.axis_index("pipe")
    ctx = lax.axis_index("ctx")
    zed = lax.axis_index("fsdp")
    on_first = core == 0
    rows = tokens.shape[2]
    width = tokens.shape[3]
    length = doc_ids.shape[2]
    kv_width = w_keyval.shape[2] // 2

    pieces = own_pieces(
        w_query[0], w_keyval[0], w_out[0], w_gateup[0], w_down[0], core, ctx
    )
    gains = jnp.concatenate([gain_attn, gain_ffn], axis=0)
    gains_other = swap_cores(gains)
    layer_gains = (pick(on_first, gains, gains_other), pick(on_first, gains_other, gains))

    doc_row = lax.dynamic_index_in_dim(doc_ids[:, 0], core, 0, keepdims=False)
    inputs_low = lax.dynamic_index_in_dim(tokens[:, 0], core, 0, keepdims=False)
    cotangent_own = lax.dynamic_index_in_dim(cotangent[:, 0], core, 0, keepdims=False)
    earlier = jnp.sum((doc_row[None, :] < doc_row[:, None]).astype(jnp.int32), axis=1)
    positions = jnp.arange(length, dtype=jnp.int32) - earlier
    token_pos = lax.dynamic_slice_in_dim(positions, ctx * rows, rows, 0)
    tables = angle_tables(token_pos.astype(F32))
    own_docs = lax.dynamic_slice_in_dim(doc_row, ctx * rows, rows, 0)
    query_index = ctx * rows + jnp.arange(rows, dtype=jnp.int32)
    key_docs = []
    key_index = []
    for mask in range(4):
        key_docs.append(lax.dynamic_slice_in_dim(doc_row, (ctx ^ mask) * rows, rows, 0))
        key_index.append((ctx ^ mask) * rows + jnp.arange(rows, dtype=jnp.int32))
    key_docs = jnp.concatenate(key_docs)
    key_index = jnp.concatenate(key_index)
    seen = (own_docs[None, :] == key_docs[:, None]) & (
        key_index[:, None] <= query_index[None, :]
    )
    bias = jnp.where(seen, 0.0, NEGATIVE).astype(F32)

    order = Order()
    (attn_first, ffn_first, down_first), (attn_second, ffn_second, down_second) = pieces
    tiles = w_gateup.shape[1] % 16 == 0
    split = attn_first.shape[0]
    attn0 = Spread(order, attn_first)
    ffn_first, down_first = order.waits((ffn_first, down_first))
    if tiles:
        down0 = Down(order, down_first)
    attn0.flights[0] = order.wait(attn0.flights[0])
    if tiles:
        ffn0 = Spread(order, ffn_first)
    attn0.advance()
    attn0.advance()
    if tiles:
        ffn0.advance()
    second = order.hold(jnp.concatenate([attn_second, ffn_second], axis=0))
    second = lax.all_gather(second, "fsdp", axis=0, tiled=False)
    attn0.advance()
    w_attn0 = order.wait(place_attn(attn0))
    own0 = project(inputs_low, w_attn0, layer_gains[0][0], tables)
    keys0 = send_keys(own0[2])
    keyval0 = (own0[2], *[order.wait(flow) for flow in keys0])
    if tiles:
        ffn0.advance()
        down0.start()
    resid0, attn_saved0 = attend(inputs_low, own0, keyval0, w_attn0, bias)
    resid0 = order.wait(resid0)
    second = order.wait(second)
    attn1 = Spread.behind(order, second[:, :split])
    attn1.advance()
    if tiles:
        down1 = Down(order, down_second)
        ffn0.advance()
        weights0 = Ffn(ffn0, down0.finish())
    else:
        weights0 = WholeFfn(w_gateup[0], w_down[0], 0)
        weights1 = WholeFfn(w_gateup[0], w_down[0], 1)
    middle, *ffn_saved0 = weights0.forward(resid0, layer_gains[0][1])
    middle = order.wait(middle)
    attn1.advance()
    if tiles:
        ffn1 = Spread.behind(order, second[:, split:])
        ffn1.advance()
    attn1.advance()
    w_attn1 = order.wait(place_attn(attn1))
    own1 = project(middle, w_attn1, layer_gains[1][0], tables)
    keys1 = send_keys(own1[2])
    if tiles:
        ffn1.advance()
    keyval1 = (own1[2], *[order.wait(flow) for flow in keys1])
    if tiles:
        down1.start()
    resid1, attn_saved1 = attend(middle, own1, keyval1, w_attn1, bias)
    resid1 = order.wait(resid1)
    turned0 = [(array, order.wait(swap_cores(array))) for array in (ffn_saved0[0], ffn_saved0[3])]
    if tiles:
        ffn1.advance()
        weights1 = Ffn(ffn1, down1.finish())
    (outputs1, normed1, hidden1), back1 = weights1.both(
        resid1, layer_gains[1][1], cotangent_own
    )
    section_outs = [middle, outputs1]

    weights = [(w_attn0, weights0), (w_attn1, weights1)]
    saved = [(attn_saved0, (resid0, *ffn_saved0)), (attn_saved1, None)]
    half = -(-width // 256) * 128
    turned = [
        turned0,
        [(array, swap_cores(array)) for array in (normed1, hidden1)],
    ]

    grad_low = cotangent_own
    input_grads = [None, None]
    reduced = [None, None]
    gain_grads = [None, None]
    above = None
    for layer in (1, 0):
        w_attn, w_ffn = weights[layer]
        attn_saved, ffn_saved = saved[layer]
        normed, hidden = turned[layer]
        grad_low = order.wait(grad_low)
        own, send = two_ways(grad_low[:, :half], grad_low[:, width - half :])
        down = Reduce(order, order.waits(term((*hidden, own, swap_cores(send), True))), True)
        if layer == 1:
            resid_grad, gain_ffn_grad, own, send = back1
        else:
            resid_grad, gain_ffn_grad, own, send = w_ffn.backward(
                order.hold(grad_low),
                ffn_saved[0],
                layer_gains[layer][1],
                ffn_saved[2],
                ffn_saved[3],
            )
        resid_grad = order.wait(resid_grad)
        if layer == 0:
            above[1].advance()
            above[2].advance()
            above[0].settle()
            down.advance()
        *rights, kv_own, kv_x, kv_y, kv_xy = backward_scores(
            resid_grad, attn_saved, w_attn, bias, tables
        )
        kv_own = order.wait(kv_own)
        flows = return_keys(order.hold(kv_x, kv_y, kv_xy))
        gateup_term = order.waits(term((*normed, own, swap_cores(send), True)))
        if layer == 0:
            above[1].advance()
        flows = [order.wait(flow) for flow in flows]
        gateup = Reduce(order, order.hold(*gateup_term), True)
        if layer == 1:
            down.advance()
        grad_low, gain_attn_grad, own, send = backward_project(
            resid_grad, rights, kv_own, flows, attn_saved, w_attn, layer_gains[layer][0], tables
        )
        gain_grads[layer] = (gain_attn_grad, gain_ffn_grad)
        gains = None
        if layer == 0:
            grad_low = order.wait(grad_low)
            gains = jnp.stack([*gain_grads[0], *gain_grads[1]])
            gains = gains + swap_cores(gains)
            gains = pick(on_first, gains[:2], gains[2:])
        lefts = attn_saved[6]
        attn = Reduce(
            order,
            order.waits(
                term(
                    (*lefts[:2], rights[0], swap_cores(rights[1]), False),
                    (*lefts[2:], own, swap_cores(send), False),
                    gains=gains,
                )
            ),
            layer == 1,
            0 if gains is None else 16,
        )
        if layer == 1:
            down.advance()
            above = [down, gateup, attn]
        reduced[layer] = [down, gateup, attn]
        input_grads[layer] = grad_low

    above[2].advance()
    down.advance()
    above[1].settle()
    gateup.advance()

    def to_layers(first, second):
        own, other = two_ways(first, second)
        other = swap_cores(other)
        return two_ways(own, other)

    section_out = order.wait(jnp.stack(to_layers(section_outs[0], section_outs[1])))
    attn.advance()
    above[2].settle()
    gateup.advance()
    section_in_grad = order.wait(jnp.stack(to_layers(input_grads[0], input_grads[1])))
    attn.advance()
    down.settle()
    down_left, down_right = order.waits(to_layers(down.result, above[0].result))
    attn.advance()
    gain_total = attn.result[-16:-14, :width]
    attn_first, attn_second = to_layers(attn.result[:-16].astype(BF16), above[2].result)
    gateup.settle()
    gate, up = to_layers(gateup.result, above[1].result)
    attn_first, attn_second, gate, up, down_left, down_right = [
        array.astype(F32) for array in (attn_first, attn_second, gate, up, down_left, down_right)
    ]
    return (
        section_out[None, :, None],
        section_in_grad[None, :, None],
        attn_first[None, :, :width],
        jnp.concatenate([attn_first[:, width:], attn_second[:, width:]], axis=1)[None],
        attn_second[None, :, :width],
        jnp.concatenate([gate, up], axis=1)[None],
        jnp.concatenate(
            [down_left[:, : width // 2], down_right[:, half - width // 2 :]], axis=1
        )[None],
        gain_total[0][None],
        gain_total[1][None],
    )


def solution(mesh):
    return jax.shard_map(
        shards,
        mesh=mesh,
        in_specs=(
            P(None, "fsdp", "ctx", None),
            P(None, "fsdp", "ctx", None),
            P(None, "fsdp", None),
            P("pipe", "fsdp", None),
            P("pipe", "fsdp", None),
            P("pipe", "fsdp", None),
            P("pipe", "fsdp", None),
            P("pipe", "fsdp", None),
            P("pipe", None),
            P("pipe", None),
        ),
        out_specs=(
            P("pipe", None, "fsdp", "ctx", None),
            P("pipe", None, "fsdp", "ctx", None),
            P("pipe", ("ctx", "fsdp"), None),
            P("pipe", ("ctx", "fsdp"), None),
            P("pipe", ("ctx", "fsdp"), None),
            P("pipe", ("ctx", "fsdp"), None),
            P("pipe", ("ctx", "fsdp"), None),
            P("pipe", None),
            P("pipe", None),
        ),
        check_vma=False,
    )
```

profile of v0, /device:TPU:0, one launch (start us, length us, event | category | flops | bytes accessed | tf_op | source)
XLA Modules:
  0.0 577.8 jit_solution(11090945970853105609)
XLA Ops:
  15.4 3.0 collective-permute-start.1
  18.4 2.6 collective-permute-start.3
  21.0 4.2 collective-permute-done.1
  25.2 11.2 %collective-permute-done.3 = bf16[1,120,640]{2,1,0:T(8,128)(2,1)S(1)} collective-permute-done((bf16[1,120,640]{2,1,0:T(8,128)(2,1)S(1)}, bf16[1,120,640]{2,1,0:T(8,128)(2,1)S(1)}, u32[]{:S(2)}, u32[]{:S(2)}) %collective-permute-start.3) | collective-permute-done | bytes 153632 | tf_op jit(solution)/shard_map/ppermute | solution.py:32
  40.9 10.4 %collective-permute-start.10 = (bf16[1,240,640]{2,1,0:T(8,128)(2,1)S(1)}, bf16[1,240,640]{2,1,0:T(8,128)(2,1)S(1)}, u32[]{:S(2)}, u32[]{:S(2)}) collective-permute-start(bf16[1,240,640]{2,1,0:T(8,128)(2,1)S(1)} %bitcast.136), channel_id=1, source_target_pairs={{0,1},{1,0},{2,3},{3,2},{4,5},{5,4},{6,7},{7,6},{8,9},{9,8},{10,11... | collective-permute-start | bytes 921608 | tf_op jit(solution)/shard_map/ppermute | solution.py:32
  51.3 2.3 collective-permute-start.9
  56.5 9.1 %collective-permute-done.10 = bf16[1,240,640]{2,1,0:T(8,128)(2,1)S(1)} collective-permute-done((bf16[1,240,640]{2,1,0:T(8,128)(2,1)S(1)}, bf16[1,240,640]{2,1,0:T(8,128)(2,1)S(1)}, u32[]{:S(2)}, u32[]{:S(2)}) %collective-permute-start.10) | collective-permute-done | bytes 307232 | tf_op jit(solution)/shard_map/ppermute | solution.py:32
  65.6 11.5 %collective-permute-done.9 = bf16[1,240,640]{2,1,0:T(8,128)(2,1)S(1)} collective-permute-done((bf16[1,240,640]{2,1,0:T(8,128)(2,1)S(1)}, bf16[1,240,640]{2,1,0:T(8,128)(2,1)S(1)}, u32[]{:S(2)}, u32[]{:S(2)}) %collective-permute-start.9) | collective-permute-done | bytes 307232 | tf_op jit(solution)/shard_map/ppermute | solution.py:32
  82.0 2.0 constant_dynamic-slice_fusion
  85.0 2.8 shard_map.169
  87.8 2.2 copy-done
  90.1 3.7 shard_map.170
  95.8 2.2 collective-permute-start.18
  98.8 14.8 %collective-permute-done.16.p1 = bf16[640,256]{1,0:T(8,128)(2,1)S(1)} collective-permute-done((bf16[640,256]{1,0:T(8,128)(2,1)S(1)}, bf16[640,256]{1,0:T(8,128)(2,1)S(1)}, u32[]{:S(2)}, u32[]{:S(2)}) %collective-permute-start.16) | collective-permute-done | bytes 327712 | tf_op jit(solution)/shard_map/ppermute | solution.py:32
  117.8 3.4 collective-permute-start.22
  126.6 12.1 %shard_map.171 = (bf16[960,256]{1,0:T(8,128)(2,1)S(1)}, bf16[960,256]{1,0:T(8,128)(2,1)S(1)}, f32[15,1,256]{2,1,0:T(1,128)S(1)}, f32[256,960]{1,0:T(8,128)S(1)}, bf16[960,256]{1,0:T(8,128)(2,1)}) custom-call(bf16[960,256]{1,0:T(8,128)(2,1)S(1)} %copy-done.40, bf16[640,256]{1,0:T(8,128)(2,1)S(1)} %copy-done.46, bf16[640,256]{1,0:T(8,128)(2,1)S(1)} %copy-done.49, ...), custom_call_target="tpu_custom_call" | custom-call | tf_op jit(solution)/shard_map/pallas_call | solution.py:651
  141.3 3.0 collective-permute-done.22.refs_3_
  152.5 12.0 %shard_map.172 = (bf16[256,960]{1,0:T(8,128)(2,1)S(1)}, bf16[960,256]{1,0:T(8,128)(2,1)S(1)}, f32[256,2560]{1,0:T(8,128)}, f32[256,2560]{1,0:T(8,128)}, bf16[2560,256]{1,0:T(8,128)(2,1)}) custom-call(f32[256,960]{1,0:T(8,128)S(1)} %copy-done.6, f32[1,960]{1,0:T(1,128)S(1)} %get-tuple-element.429.gain_ref, bf16[4,240,640]{2,1,0:T(8,128)(2,1)S(1)} %pad_maximum_fusion.refs_0_, ...), custom_call_target="tpu_custom_call" | custom-call | tf_op jit(solution)/shard_map/pallas_call | solution.py:294
  164.5 2.2 collective-permute-start.32
  168.8 12.5 %collective-permute-done.32.refs_3_ = bf16[4,120,640]{2,1,0:T(8,128)(2,1)S(1)} collective-permute-done((bf16[4,120,640]{2,1,0:T(8,128)(2,1)}, bf16[4,120,640]{2,1,0:T(8,128)(2,1)S(1)}, u32[]{:S(2)}, u32[]{:S(2)}) %collective-permute-start.32) | collective-permute-done | bytes 614432 | tf_op jit(solution)/shard_map/ppermute | solution.py:71
  181.8 2.5 collective-permute-done.34.refs_5_
  186.2 2.3 copy-done.1
  188.5 3.7 shard_map.174
  194.9 2.2 collective-permute-start.40
  198.4 6.7 %collective-permute-done.38.refs_2_ = bf16[4,240,640]{2,1,0:T(8,128)(2,1)} collective-permute-done((bf16[4,240,640]{2,1,0:T(8,128)(2,1)S(1)}, bf16[4,240,640]{2,1,0:T(8,128)(2,1)}, u32[]{:S(2)}, u32[]{:S(2)}) %collective-permute-start.38) | collective-permute-done | bytes 1228832 | tf_op jit(solution)/shard_map/ppermute | solution.py:71
  205.1 2.8 collective-permute-start.42
  208.5 6.3 %collective-permute-done.40.p2 = bf16[640,256]{1,0:T(8,128)(2,1)S(1)} collective-permute-done((bf16[640,256]{1,0:T(8,128)(2,1)S(1)}, bf16[640,256]{1,0:T(8,128)(2,1)S(1)}, u32[]{:S(2)}, u32[]{:S(2)}) %collective-permute-start.40) | collective-permute-done | bytes 327712 | tf_op jit(solution)/shard_map/ppermute | solution.py:32
  223.9 12.4 %shard_map.175 = (bf16[960,256]{1,0:T(8,128)(2,1)S(1)}, bf16[960,256]{1,0:T(8,128)(2,1)}, f32[15,1,256]{2,1,0:T(1,128)S(1)}, f32[256,960]{1,0:T(8,128)S(1)}, bf16[960,256]{1,0:T(8,128)(2,1)}) custom-call(bf16[960,256]{1,0:T(8,128)(2,1)S(1)} %copy-done.43, bf16[640,256]{1,0:T(8,128)(2,1)S(1)} %copy-done.58, bf16[640,256]{1,0:T(8,128)(2,1)S(1)} %copy-done.61, ...), custom_call_target="tpu_custom_call" | custom-call | tf_op jit(solution)/shard_map/pallas_call | solution.py:651
  243.6 2.0 copy.36
  252.3 19.6 %shard_map.176 = (bf16[256,960]{1,0:T(8,128)(2,1)S(1)}, bf16[960,256]{1,0:T(8,128)(2,1)S(1)}, bf16[2560,256]{1,0:T(8,128)(2,1)}, f32[256,960]{1,0:T(8,128)S(1)},...) custom-call(f32[256,960]{1,0:T(8,128)S(1)} %copy-done.82, ...), custom_call_target="tpu_custom_call" | custom-call | tf_op jit(solution)/shard_map/pallas_call | solution.py:294
  273.9 3.9 collective-permute-done.54.refs_3_
  282.4 21.2 %shard_map.178 = (bf16[960,256]{1,0:T(8,128)(2,1)S(1)}, bf16[960,256]{1,0:T(8,128)(2,1)}, f32[640,256]{1,0:T(8,128)}, bf16[640,256]{1,0:T(8,128)(2,1)S(1)}, bf16...) custom-call(f32[256,960]{1,0:T(8,128)} %copy-done.8, ...), custom_call_target="tpu_custom_call" | custom-call | tf_op jit(solution)/shard_map/pallas_call | solution.py:651
  305.4 2.5 collective-permute-start.58
  308.3 5.4 shard_map.179
  315.4 6.3 %collective-permute-done.58.kv2 = bf16[640,256]{1,0:T(8,128)(2,1)S(1)} collective-permute-done((bf16[640,256]{1,0:T(8,128)(2,1)S(1)}, bf16[640,256]{1,0:T(8,128)(2,1)S(1)}, u32[]{:S(2)}, u32[]{:S(2)}) %collective-permute-start.58) | collective-permute-done | bytes 327712 | tf_op jit(solution)/shard_map/ppermute | solution.py:32
  324.9 2.4 fusion.8
  333.3 4.1 shard_map.180
  344.7 3.4 shard_map.181
  348.1 3.2 fusion.4
  354.0 4.1 shard_map.182
  359.1 13.4 %shard_map.183 = (f32[256,960]{1,0:T(8,128)S(1)}, f32[1,960]{1,0:T(1,128)S(1)}, bf16[256,2560]{1,0:T(8,128)(2,1)}, bf16[256,2560]{1,0:T(8,128)(2,1)}) custom-call(bf16[256,960]{1,0:T(8,128)(2,1)S(1)} %get-tuple-element.291.grad_ref, f32[256,960]{1,0:T(8,128)S(1)} %copy-done.7, f32[1,960]{1,0:T(1,128)S(1)} %get-tuple-element.429.gain_ref, ...), custom_call_target="tpu_custom_call" | custom-call | tf_op jit(solution)/shard_map/pallas_call | solution.py:294
  372.8 3.2 fusion.5
  377.0 21.7 %shard_map.185 = (bf16[960,256]{1,0:T(8,128)(2,1)S(1)}, bf16[960,256]{1,0:T(8,128)(2,1)S(1)}, f32[640,256]{1,0:T(8,128)}, bf16[640,256]{1,0:T(8,128)(2,1)}, bf16...) custom-call(f32[256,960]{1,0:T(8,128)} %copy-done.10, ...), custom_call_target="tpu_custom_call" | custom-call | tf_op jit(solution)/shard_map/pallas_call | solution.py:651
  400.4 2.1 fusion.12
  402.5 2.4 fusion.9
  404.9 6.1 %shard_map.184 = (bf16[2,240,2560]{2,1,0:T(8,128)(2,1)S(1)}, bf16[2,240,2560]{2,1,0:T(8,128)(2,1)}) custom-call(bf16[960,256]{1,0:T(8,128)(2,1)S(1)} %copy-done.86, bf16[960,256]{1,0:T(8,128)(2,1)S(1)} %copy-done.88, bf16[256,2560]{1,0:T(8,128)(2,1)S(1)} %copy-done.70, bf16[256,2560]{1,0:T(8,128)(2,1)} %collective-permute-done.67.refs_3_), custom_call_target="tpu_custom_call" | custom-call | tf_op jit(solution)/shard_map/pallas_call | solution.py:651
  414.6 3.1 fusion.1
  417.7 2.3 reshape.120
  422.6 6.4 %collective-permute-done.72.kv2 = bf16[640,256]{1,0:T(8,128)(2,1)} collective-permute-done((bf16[640,256]{1,0:T(8,128)(2,1)}, bf16[640,256]{1,0:T(8,128)(2,1)}, u32[]{:S(2)}, u32[]{:S(2)}) %collective-permute-start.72) | collective-permute-done | bytes 327712 | tf_op jit(solution)/shard_map/ppermute | solution.py:32
  434.0 4.5 shard_map.186
  445.0 3.1 shard_map.187
  450.3 7.1 %collective-permute-done.77 = bf16[240,1280]{1,0:T(8,128)(2,1)S(1)} collective-permute-done((bf16[240,1280]{1,0:T(8,128)(2,1)S(1)}, bf16[240,1280]{1,0:T(8,128)(2,1)S(1)}, u32[]{:S(2)}, u32[]{:S(2)}) %collective-permute-start.77) | collective-permute-done | bytes 614432 | tf_op jit(solution)/shard_map/ppermute | solution.py:71
  457.4 2.1 fusion.7
  459.5 2.1 reshape.121
  461.7 9.8 %collective-permute-done.76 = bf16[640,512]{1,0:T(8,128)(2,1)} collective-permute-done((bf16[640,512]{1,0:T(8,128)(2,1)}, bf16[640,512]{1,0:T(8,128)(2,1)}, u32[]{:S(2)}, u32[]{:S(2)}) %collective-permute-start.76) | collective-permute-done | bytes 655392 | tf_op jit(solution)/shard_map/ppermute | solution.py:71
  471.5 2.4 fusion.3
  473.9 3.0 fusion.6
  483.0 11.4 %collective-permute-done.85 = bf16[2,256,1280]{2,1,0:T(8,128)(2,1)} collective-permute-done((bf16[2,256,1280]{2,1,0:T(8,128)(2,1)}, bf16[2,256,1280]{2,1,0:T(8,128)(2,1)}, u32[]{:S(2)}, u32[]{:S(2)}) %collective-permute-start.85) | collective-permute-done | bytes 1310752 | tf_op jit(solution)/shard_map/ppermute | solution.py:66
  497.5 2.5 fusion
  501.4 5.0 collective-permute-done.86
  509.0 7.9 %reduce-scatter.12.cloned.1.call-done = bf16[1,160,512]{2,1,0:T(8,128)(2,1)} async-done(((bf16[4,160,512]{2,1,0:T(8,128)(2,1)}), bf16[1,160,512]{2,1,0:T(8,128)(2,1)}) %reduce-scatter.12.cloned.1.call-update) | async-done | bytes 163856 | tf_op jit(solution)/shard_map/reduce_scatter | solution.py:613
  520.3 5.1 collective-permute-start.89
  528.9 32.1 %collective-permute-done.89 = bf16[76,1280]{1,0:T(8,128)(2,1)} collective-permute-done((bf16[76,1280]{1,0:T(8,128)(2,1)S(1)}, bf16[76,1280]{1,0:T(8,128)(2,1)}, u32[]{:S(2)}, u32[]{:S(2)}) %collective-permute-start.89) | collective-permute-done | bytes 194592 | tf_op jit(solution)/shard_map/ppermute | solution.py:32
  568.2 2.3 copy.42
  (516 shorter events, 156.2 us)
Async XLA Ops:
  7.2 114.0 %all-gather.7.cloned.1.call-start = ((), (), s32[]{:S(2)}) async-start(), calls=%async_computation.10 | async-start | bytes 1638400 | tf_op jit(solution)/shard_map/all_gather | solution.py:232
  13.4 127.9 %all-gather.9.cloned.1.call-start = ((), (), s32[]{:S(2)}) async-start(), calls=%async_computation.11 | async-start | bytes 2304000 | tf_op jit(solution)/shard_map/all_gather | solution.py:958
  18.4 18.0 %collective-permute-start.3 = (bf16[1,120,640]{2,1,0:T(8,128)(2,1)S(1)}, bf16[1,120,640]{2,1,0:T(8,128)(2,1)S(1)}, u32[]{:S(2)}, u32[]{:S(2)}) collective-permute-start(bf16[1,120,640]{2,1,0:T(8,128)(2,1)S(1)} %get-tuple-element.422), channel_id=1, source_target_pairs={{0,2},{1,3},{2,0},{3,1},{4,6},{5,7},{6,4},{7,5},{8,10},{9,11},{10,... | collective-permute-start | bytes 460808 | tf_op jit(solution)/shard_map/ppermute | solution.py:32
  21.0 15.4 %collective-permute-start.4 = (bf16[1,120,640]{2,1,0:T(8,128)(2,1)S(1)}, bf16[1,120,640]{2,1,0:T(8,128)(2,1)S(1)}, u32[]{:S(2)}, u32[]{:S(2)}) collective-permute-start(bf16[1,120,640]{2,1,0:T(8,128)(2,1)S(1)} %get-tuple-element.422), channel_id=1, source_target_pairs={{0,3},{1,2},{2,1},{3,0},{4,7},{5,6},{6,5},{7,4},{8,11},{9,10},{10,... | collective-permute-start | bytes 460808 | tf_op jit(solution)/shard_map/ppermute | solution.py:32
  37.3 17.7 %collective-permute-start.5 = (bf16[4,120,640]{2,1,0:T(8,128)(2,1)}, bf16[4,120,640]{2,1,0:T(8,128)(2,1)}, u32[]{:S(2)}, u32[]{:S(2)}) collective-permute-start(bf16[4,120,640]{2,1,0:T(8,128)(2,1)} %pad_maximum_fusion.3.refs_0_), channel_id=1, source_target_pairs={{0,4},{4,0},{8,12},{12,8},{16,24},{20,28},{24,16},{28,20},{1,5},{5... | collective-permute-start | bytes 1843208 | tf_op jit(solution)/shard_map/ppermute | solution.py:66
  38.8 16.2 %collective-permute-start.6 = (bf16[4,120,640]{2,1,0:T(8,128)(2,1)}, bf16[4,120,640]{2,1,0:T(8,128)(2,1)}, u32[]{:S(2)}, u32[]{:S(2)}) collective-permute-start(bf16[4,120,640]{2,1,0:T(8,128)(2,1)} %pad_maximum_fusion.3.refs_0_), channel_id=1, source_target_pairs={{0,8},{4,12},{8,0},{12,4},{16,20},{20,16},{24,28},{28,24},{1,9},{5... | collective-permute-start | bytes 1843208 | tf_op jit(solution)/shard_map/ppermute | solution.py:71
  40.9 24.7 %collective-permute-start.10 = (bf16[1,240,640]{2,1,0:T(8,128)(2,1)S(1)}, bf16[1,240,640]{2,1,0:T(8,128)(2,1)S(1)}, u32[]{:S(2)}, u32[]{:S(2)}) collective-permute-start(bf16[1,240,640]{2,1,0:T(8,128)(2,1)S(1)} %bitcast.136), channel_id=1, source_target_pairs={{0,1},{1,0},{2,3},{3,2},{4,5},{5,4},{6,7},{7,6},{8,9},{9,8},{10,11... | collective-permute-start | bytes 921608 | tf_op jit(solution)/shard_map/ppermute | solution.py:32
  51.3 25.8 %collective-permute-start.9 = (bf16[1,240,640]{2,1,0:T(8,128)(2,1)S(1)}, bf16[1,240,640]{2,1,0:T(8,128)(2,1)S(1)}, u32[]{:S(2)}, u32[]{:S(2)}) collective-permute-start(bf16[1,240,640]{2,1,0:T(8,128)(2,1)S(1)} %bitcast.137), channel_id=1, source_target_pairs={{0,2},{1,3},{2,0},{3,1},{4,6},{5,7},{6,4},{7,5},{8,10},{9,11},{10,... | collective-permute-start | bytes 921608 | tf_op jit(solution)/shard_map/ppermute | solution.py:32
  53.6 23.5 %collective-permute-start.8 = (bf16[1,240,640]{2,1,0:T(8,128)(2,1)S(1)}, bf16[1,240,640]{2,1,0:T(8,128)(2,1)S(1)}, u32[]{:S(2)}, u32[]{:S(2)}) collective-permute-start(bf16[1,240,640]{2,1,0:T(8,128)(2,1)S(1)} %bitcast.138), channel_id=1, source_target_pairs={{0,3},{1,2},{2,1},{3,0},{4,7},{5,6},{6,5},{7,4},{8,11},{9,10},{10,... | collective-permute-start | bytes 921608 | tf_op jit(solution)/shard_map/ppermute | solution.py:32
  55.0 26.4 %collective-permute-start.11 = (bf16[4,120,640]{2,1,0:T(8,128)(2,1)}, bf16[4,120,640]{2,1,0:T(8,128)(2,1)}, u32[]{:S(2)}, u32[]{:S(2)}) collective-permute-start(bf16[4,120,640]{2,1,0:T(8,128)(2,1)} %pad_maximum_fusion.3.refs_0_), channel_id=1, source_target_pairs={{0,16},{16,0},{1,17},{17,1},{2,18},{18,2},{3,19},{19,3},{4,20},{20... | collective-permute-start | bytes 1843208 | tf_op jit(solution)/shard_map/ppermute | solution.py:23
  55.0 25.8 %collective-permute-start.7 = (bf16[4,120,640]{2,1,0:T(8,128)(2,1)}, bf16[4,120,640]{2,1,0:T(8,128)(2,1)}, u32[]{:S(2)}, u32[]{:S(2)}) collective-permute-start(bf16[4,120,640]{2,1,0:T(8,128)(2,1)} %collective-permute-done.5.refs_1_), channel_id=1, source_target_pairs={{0,8},{4,12},{8,0},{12,4},{16,20},{20,16},{24,28},{28,24},{1,9},{5... | collective-permute-start | bytes 1843208 | tf_op jit(solution)/shard_map/ppermute | solution.py:71
  65.6 15.3 %collective-permute-start.15 = (f32[2,960]{1,0:T(2,128)S(1)}, f32[2,960]{1,0:T(2,128)S(1)}, u32[]{:S(2)}, u32[]{:S(2)}) collective-permute-start(f32[2,960]{1,0:T(2,128)S(1)} %pad_maximum_fusion.8), channel_id=1, source_target_pairs={{0,16},{16,0},{1,17},{17,1},{2,18},{18,2},{3,19},{19,3},{4,20},{20... | collective-permute-start | bytes 23048 | tf_op jit(solution)/shard_map/ppermute | solution.py:23
  77.1 139.2 %all-gather.11.cloned.1.call-start = ((), (), s32[]{:S(2)}) async-start(), calls=%async_computation.12 | async-start | bytes 1638400 | tf_op jit(solution)/shard_map/all_gather | solution.py:232
  77.5 40.3 %collective-permute-start.21 = (bf16[4,240,640]{2,1,0:T(8,128)(2,1)S(1)}, bf16[4,240,640]{2,1,0:T(8,128)(2,1)S(1)}, u32[]{:S(2)}, u32[]{:S(2)}) collective-permute-start(bf16[4,240,640]{2,1,0:T(8,128)(2,1)S(1)} %pad_maximum_fusion.refs_0_), channel_id=1, source_target_pairs={{0,4},{4,0},{8,12},{12,8},{16,24},{20,28},{24,16},{28,20},{1,5},{5... | collective-permute-start | bytes 3686408 | tf_op jit(solution)/shard_map/ppermute | solution.py:66
  79.3 41.9 %collective-permute-start.20 = (bf16[4,240,640]{2,1,0:T(8,128)(2,1)S(1)}, bf16[4,240,640]{2,1,0:T(8,128)(2,1)}, u32[]{:S(2)}, u32[]{:S(2)}) collective-permute-start(bf16[4,240,640]{2,1,0:T(8,128)(2,1)S(1)} %pad_maximum_fusion.refs_0_), channel_id=1, source_target_pairs={{0,8},{4,12},{8,0},{12,4},{16,20},{20,16},{24,28},{28,24},{1,9},{5... | collective-permute-start | bytes 3686408 | tf_op jit(solution)/shard_map/ppermute | solution.py:71
  94.6 19.0 %collective-permute-start.16 = (bf16[640,256]{1,0:T(8,128)(2,1)S(1)}, bf16[640,256]{1,0:T(8,128)(2,1)S(1)}, u32[]{:S(2)}, u32[]{:S(2)}) collective-permute-start(bf16[640,256]{1,0:T(8,128)(2,1)S(1)} %get-tuple-element.204.p0), channel_id=1, source_target_pairs={{0,4},{4,0},{8,12},{12,8},{1,5},{5,1},{9,13},{13,9},{2,6},{6,2},{1... | collective-permute-start | bytes 983048 | tf_op jit(solution)/shard_map/ppermute | solution.py:32
  95.4 18.9 %collective-permute-start.17 = (bf16[640,256]{1,0:T(8,128)(2,1)S(1)}, bf16[640,256]{1,0:T(8,128)(2,1)S(1)}, u32[]{:S(2)}, u32[]{:S(2)}) collective-permute-start(bf16[640,256]{1,0:T(8,128)(2,1)S(1)} %get-tuple-element.204.p0), channel_id=1, source_target_pairs={{0,8},{4,12},{8,0},{12,4},{1,9},{5,13},{9,1},{13,5},{2,10},{6,14},... | collective-permute-start | bytes 983048 | tf_op jit(solution)/shard_map/ppermute | solution.py:32
  95.8 21.3 %collective-permute-start.18 = (bf16[640,256]{1,0:T(8,128)(2,1)S(1)}, bf16[640,256]{1,0:T(8,128)(2,1)S(1)}, u32[]{:S(2)}, u32[]{:S(2)}) collective-permute-start(bf16[640,256]{1,0:T(8,128)(2,1)S(1)} %get-tuple-element.204.p0), channel_id=1, source_target_pairs={{0,12},{4,8},{8,4},{12,0},{1,13},{5,9},{9,5},{13,1},{2,14},{6,10},... | collective-permute-start | bytes 983048 | tf_op jit(solution)/shard_map/ppermute | solution.py:32
  117.8 26.6 %collective-permute-start.22 = (bf16[4,240,640]{2,1,0:T(8,128)(2,1)S(1)}, bf16[4,240,640]{2,1,0:T(8,128)(2,1)}, u32[]{:S(2)}, u32[]{:S(2)}) collective-permute-start(bf16[4,240,640]{2,1,0:T(8,128)(2,1)S(1)} %collective-permute-done.21.refs_1_), channel_id=1, source_target_pairs={{0,8},{4,12},{8,0},{12,4},{16,20},{20,16},{24,28},{28,24},{1,9},{5... | collective-permute-start | bytes 3686408 | tf_op jit(solution)/shard_map/ppermute | solution.py:71
  121.2 23.3 %collective-permute-start.27 = (bf16[4,160,960]{2,1,0:T(8,128)(2,1)}, bf16[4,160,960]{2,1,0:T(8,128)(2,1)}, u32[]{:S(2)}, u32[]{:S(2)}) collective-permute-start(bf16[4,160,960]{2,1,0:T(8,128)(2,1)} %bitcast.122), channel_id=1, source_target_pairs={{0,4},{4,0},{8,12},{12,8},{16,24},{20,28},{24,16},{28,20},{1,5},{5... | collective-permute-start | bytes 3686408 | tf_op jit(solution)/shard_map/ppermute | solution.py:66
  121.6 23.3 %collective-permute-start.23 = (bf16[4,240,640]{2,1,0:T(8,128)(2,1)S(1)}, bf16[4,240,640]{2,1,0:T(8,128)(2,1)}, u32[]{:S(2)}, u32[]{:S(2)}) collective-permute-start(bf16[4,240,640]{2,1,0:T(8,128)(2,1)S(1)} %pad_maximum_fusion.refs_0_), channel_id=1, source_target_pairs={{0,16},{16,0},{1,17},{17,1},{2,18},{18,2},{3,19},{19,3},{4,20},{20... | collective-permute-start | bytes 3686408 | tf_op jit(solution)/shard_map/ppermute | solution.py:23
  121.6 25.3 %collective-permute-start.28 = (bf16[4,160,960]{2,1,0:T(8,128)(2,1)}, bf16[4,160,960]{2,1,0:T(8,128)(2,1)}, u32[]{:S(2)}, u32[]{:S(2)}) collective-permute-start(bf16[4,160,960]{2,1,0:T(8,128)(2,1)} %bitcast.123), channel_id=1, source_target_pairs={{0,16},{16,0},{1,17},{17,1},{2,18},{18,2},{3,19},{19,3},{4,20},{20... | collective-permute-start | bytes 3686408 | tf_op jit(solution)/shard_map/ppermute | solution.py:23
  122.2 26.5 %collective-permute-start.25 = (bf16[4,240,640]{2,1,0:T(8,128)(2,1)}, bf16[4,240,640]{2,1,0:T(8,128)(2,1)}, u32[]{:S(2)}, u32[]{:S(2)}) collective-permute-start(bf16[4,240,640]{2,1,0:T(8,128)(2,1)} %collective-permute-done.20.refs_2_), channel_id=1, source_target_pairs={{0,16},{16,0},{1,17},{17,1},{2,18},{18,2},{3,19},{19,3},{4,20},{20... | collective-permute-start | bytes 3686408 | tf_op jit(solution)/shard_map/ppermute | solution.py:23
  146.9 17.6 %collective-permute-start.30 = (bf16[4,120,640]{2,1,0:T(8,128)(2,1)}, bf16[4,120,640]{2,1,0:T(8,128)(2,1)}, u32[]{:S(2)}, u32[]{:S(2)}) collective-permute-start(bf16[4,120,640]{2,1,0:T(8,128)(2,1)} %slice.104.refs_0_), channel_id=1, source_target_pairs={{0,4},{4,0},{8,12},{12,8},{16,24},{20,28},{24,16},{28,20},{1,5},{5... | collective-permute-start | bytes 1843208 | tf_op jit(solution)/shard_map/ppermute | solution.py:66
  148.7 18.1 %collective-permute-start.31 = (bf16[4,120,640]{2,1,0:T(8,128)(2,1)}, bf16[4,120,640]{2,1,0:T(8,128)(2,1)}, u32[]{:S(2)}, u32[]{:S(2)}) collective-permute-start(bf16[4,120,640]{2,1,0:T(8,128)(2,1)} %slice.104.refs_0_), channel_id=1, source_target_pairs={{0,8},{4,12},{8,0},{12,4},{16,20},{20,16},{24,28},{28,24},{1,9},{5... | collective-permute-start | bytes 1843208 | tf_op jit(solution)/shard_map/ppermute | solution.py:71
  150.2 252.3 %reduce-scatter.6.cloned.1.call-start = ((), (), s32[]{:S(2)}) async-start(), calls=%async_computation.5 | async-start | bytes 819200 | tf_op jit(solution)/shard_map/reduce_scatter | solution.py:613
  164.5 16.8 %collective-permute-start.32 = (bf16[4,120,640]{2,1,0:T(8,128)(2,1)}, bf16[4,120,640]{2,1,0:T(8,128)(2,1)S(1)}, u32[]{:S(2)}, u32[]{:S(2)}) collective-permute-start(bf16[4,120,640]{2,1,0:T(8,128)(2,1)} %collective-permute-done.30.refs_1_), channel_id=1, source_target_pairs={{0,8},{4,12},{8,0},{12,4},{16,20},{20,16},{24,28},{28,24},{1,9},{5... | collective-permute-start | bytes 1843208 | tf_op jit(solution)/shard_map/ppermute | solution.py:71
  166.7 14.6 %collective-permute-start.33 = (bf16[4,120,640]{2,1,0:T(8,128)(2,1)}, bf16[4,120,640]{2,1,0:T(8,128)(2,1)S(1)}, u32[]{:S(2)}, u32[]{:S(2)}) collective-permute-start(bf16[4,120,640]{2,1,0:T(8,128)(2,1)} %slice.104.refs_0_), channel_id=1, source_target_pairs={{0,16},{16,0},{1,17},{17,1},{2,18},{18,2},{3,19},{19,3},{4,20},{20... | collective-permute-start | bytes 1843208 | tf_op jit(solution)/shard_map/ppermute | solution.py:23
  166.8 31.6 %collective-permute-start.39 = (bf16[4,240,640]{2,1,0:T(8,128)(2,1)S(1)}, bf16[4,240,640]{2,1,0:T(8,128)(2,1)}, u32[]{:S(2)}, u32[]{:S(2)}) collective-permute-start(bf16[4,240,640]{2,1,0:T(8,128)(2,1)S(1)} %slice.106.refs_0_), channel_id=1, source_target_pairs={{0,4},{4,0},{8,12},{12,8},{16,24},{20,28},{24,16},{28,20},{1,5},{5... | collective-permute-start | bytes 3686408 | tf_op jit(solution)/shard_map/ppermute | solution.py:66
  167.9 37.1 %collective-permute-start.38 = (bf16[4,240,640]{2,1,0:T(8,128)(2,1)S(1)}, bf16[4,240,640]{2,1,0:T(8,128)(2,1)}, u32[]{:S(2)}, u32[]{:S(2)}) collective-permute-start(bf16[4,240,640]{2,1,0:T(8,128)(2,1)S(1)} %slice.106.refs_0_), channel_id=1, source_target_pairs={{0,8},{4,12},{8,0},{12,4},{16,20},{20,16},{24,28},{28,24},{1,9},{5... | collective-permute-start | bytes 3686408 | tf_op jit(solution)/shard_map/ppermute | solution.py:71
  193.8 14.0 %collective-permute-start.37 = (bf16[640,256]{1,0:T(8,128)(2,1)S(1)}, bf16[640,256]{1,0:T(8,128)(2,1)S(1)}, u32[]{:S(2)}, u32[]{:S(2)}) collective-permute-start(bf16[640,256]{1,0:T(8,128)(2,1)S(1)} %get-tuple-element.228.p0), channel_id=1, source_target_pairs={{0,4},{4,0},{8,12},{12,8},{1,5},{5,1},{9,13},{13,9},{2,6},{6,2},{1... | collective-permute-start | bytes 983048 | tf_op jit(solution)/shard_map/ppermute | solution.py:32
  194.9 20.0 %collective-permute-start.40 = (bf16[640,256]{1,0:T(8,128)(2,1)S(1)}, bf16[640,256]{1,0:T(8,128)(2,1)S(1)}, u32[]{:S(2)}, u32[]{:S(2)}) collective-permute-start(bf16[640,256]{1,0:T(8,128)(2,1)S(1)} %get-tuple-element.228.p0), channel_id=1, source_target_pairs={{0,8},{4,12},{8,0},{12,4},{1,9},{5,13},{9,1},{13,5},{2,10},{6,14},... | collective-permute-start | bytes 983048 | tf_op jit(solution)/shard_map/ppermute | solution.py:32
  197.1 18.5 %collective-permute-start.41 = (bf16[640,256]{1,0:T(8,128)(2,1)S(1)}, bf16[640,256]{1,0:T(8,128)(2,1)S(1)}, u32[]{:S(2)}, u32[]{:S(2)}) collective-permute-start(bf16[640,256]{1,0:T(8,128)(2,1)S(1)} %get-tuple-element.228.p0), channel_id=1, source_target_pairs={{0,12},{4,8},{8,4},{12,0},{1,13},{5,9},{9,5},{13,1},{2,14},{6,10},... | collective-permute-start | bytes 983048 | tf_op jit(solution)/shard_map/ppermute | solution.py:32
  198.4 41.1 %collective-permute-start.43 = (bf16[2560,256]{1,0:T(8,128)(2,1)}, bf16[2560,256]{1,0:T(8,128)(2,1)}, u32[]{:S(2)}, u32[]{:S(2)}) collective-permute-start(bf16[2560,256]{1,0:T(8,128)(2,1)} %get-tuple-element.240.refs_0_), channel_id=1, source_target_pairs={{0,16},{16,0},{1,17},{17,1},{2,18},{18,2},{3,19},{19,3},{4,20},{20... | collective-permute-start | bytes 3932168 | tf_op jit(solution)/shard_map/ppermute | solution.py:23
  205.1 35.0 %collective-permute-start.42 = (bf16[4,240,640]{2,1,0:T(8,128)(2,1)}, bf16[4,240,640]{2,1,0:T(8,128)(2,1)}, u32[]{:S(2)}, u32[]{:S(2)}) collective-permute-start(bf16[4,240,640]{2,1,0:T(8,128)(2,1)} %collective-permute-done.39.refs_1_), channel_id=1, source_target_pairs={{0,8},{4,12},{8,0},{12,4},{16,20},{20,16},{24,28},{28,24},{1,9},{5... | collective-permute-start | bytes 3686408 | tf_op jit(solution)/shard_map/ppermute | solution.py:71
  216.3 25.5 %collective-permute-start.49 = (bf16[4,160,960]{2,1,0:T(8,128)(2,1)}, bf16[4,160,960]{2,1,0:T(8,128)(2,1)}, u32[]{:S(2)}, u32[]{:S(2)}) collective-permute-start(bf16[4,160,960]{2,1,0:T(8,128)(2,1)} %bitcast.19.refs_8_), channel_id=1, source_target_pairs={{0,4},{4,0},{8,12},{12,8},{16,24},{20,28},{24,16},{28,20},{1,5},{5... | collective-permute-start | bytes 3686408 | tf_op jit(solution)/shard_map/ppermute | solution.py:66
  217.5 25.1 %collective-permute-start.45 = (bf16[4,240,640]{2,1,0:T(8,128)(2,1)S(1)}, bf16[4,240,640]{2,1,0:T(8,128)(2,1)S(1)}, u32[]{:S(2)}, u32[]{:S(2)}) collective-permute-start(bf16[4,240,640]{2,1,0:T(8,128)(2,1)S(1)} %slice.106.refs_0_), channel_id=1, source_target_pairs={{0,16},{16,0},{1,17},{17,1},{2,18},{18,2},{3,19},{19,3},{4,20},{20... | collective-permute-start | bytes 3686408 | tf_op jit(solution)/shard_map/ppermute | solution.py:23
  217.5 21.3 %collective-permute-start.44 = (bf16[960,256]{1,0:T(8,128)(2,1)}, bf16[960,256]{1,0:T(8,128)(2,1)S(1)}, u32[]{:S(2)}, u32[]{:S(2)}) collective-permute-start(bf16[960,256]{1,0:T(8,128)(2,1)} %copy-done.85), channel_id=1, source_target_pairs={{0,16},{16,0},{1,17},{17,1},{2,18},{18,2},{3,19},{19,3},{4,20},{20... | collective-permute-start | bytes 1474568 | tf_op jit(solution)/shard_map/ppermute | solution.py:23
  272.8 35.5 %collective-permute-start.57 = (bf16[256,2560]{1,0:T(8,128)(2,1)}, bf16[256,2560]{1,0:T(8,128)(2,1)S(1)}, u32[]{:S(2)}, u32[]{:S(2)}) collective-permute-start(bf16[256,2560]{1,0:T(8,128)(2,1)} %get-tuple-element.267), channel_id=1, source_target_pairs={{0,16},{16,0},{1,17},{17,1},{2,18},{18,2},{3,19},{19,3},{4,20},{20... | collective-permute-start | bytes 3932168 | tf_op jit(solution)/shard_map/ppermute | solution.py:23
  273.2 34.7 %collective-permute-start.56 = (bf16[960,256]{1,0:T(8,128)(2,1)S(1)}, bf16[960,256]{1,0:T(8,128)(2,1)S(1)}, u32[]{:S(2)}, u32[]{:S(2)}) collective-permute-start(bf16[960,256]{1,0:T(8,128)(2,1)S(1)} %get-tuple-element.265.refs_0_), channel_id=1, source_target_pairs={{0,16},{16,0},{1,17},{17,1},{2,18},{18,2},{3,19},{19,3},{4,20},{20... | collective-permute-start | bytes 1474568 | tf_op jit(solution)/shard_map/ppermute | solution.py:23
  281.2 43.6 %collective-permute-start.60 = (bf16[2,640,512]{2,1,0:T(8,128)(2,1)}, bf16[2,640,512]{2,1,0:T(8,128)(2,1)}, u32[]{:S(2)}, u32[]{:S(2)}) collective-permute-start(bf16[2,640,512]{2,1,0:T(8,128)(2,1)} %get-tuple-element.252), channel_id=1, source_target_pairs={{0,4},{4,0},{8,12},{12,8},{16,24},{20,28},{24,16},{28,20},{1,5},{5... | collective-permute-start | bytes 3932168 | tf_op jit(solution)/shard_map/ppermute | solution.py:66
  305.4 16.3 %collective-permute-start.58 = (bf16[640,256]{1,0:T(8,128)(2,1)S(1)}, bf16[640,256]{1,0:T(8,128)(2,1)S(1)}, u32[]{:S(2)}, u32[]{:S(2)}) collective-permute-start(bf16[640,256]{1,0:T(8,128)(2,1)S(1)} %get-tuple-element.272), channel_id=1, source_target_pairs={{0,8},{4,12},{8,0},{12,4},{1,9},{5,13},{9,1},{13,5},{2,10},{6,14},... | collective-permute-start | bytes 983048 | tf_op jit(solution)/shard_map/ppermute | solution.py:32
  307.9 15.2 %collective-permute-start.59 = (bf16[640,256]{1,0:T(8,128)(2,1)S(1)}, bf16[640,256]{1,0:T(8,128)(2,1)S(1)}, u32[]{:S(2)}, u32[]{:S(2)}) collective-permute-start(bf16[640,256]{1,0:T(8,128)(2,1)S(1)} %get-tuple-element.274), channel_id=1, source_target_pairs={{0,12},{4,8},{8,4},{12,0},{1,13},{5,9},{9,5},{13,1},{2,14},{6,10},... | collective-permute-start | bytes 983048 | tf_op jit(solution)/shard_map/ppermute | solution.py:32
  323.8 49.0 %collective-permute-start.70 = (bf16[2,240,2560]{2,1,0:T(8,128)(2,1)}, bf16[2,240,2560]{2,1,0:T(8,128)(2,1)}, u32[]{:S(2)}, u32[]{:S(2)}) collective-permute-start(bf16[2,240,2560]{2,1,0:T(8,128)(2,1)} %get-tuple-element.308), channel_id=1, source_target_pairs={{0,4},{4,0},{8,12},{12,8},{16,24},{20,28},{24,16},{28,20},{1,5},{5... | collective-permute-start | bytes 7372808 | tf_op jit(solution)/shard_map/ppermute | solution.py:66
  324.9 13.3 %collective-permute-start.64 = (bf16[960,256]{1,0:T(8,128)(2,1)S(1)}, bf16[960,256]{1,0:T(8,128)(2,1)S(1)}, u32[]{:S(2)}, u32[]{:S(2)}) collective-permute-start(bf16[960,256]{1,0:T(8,128)(2,1)S(1)} %copy-done.29), channel_id=1, source_target_pairs={{0,16},{16,0},{1,17},{17,1},{2,18},{18,2},{3,19},{19,3},{4,20},{20... | collective-permute-start | bytes 1474568 | tf_op jit(solution)/shard_map/ppermute | solution.py:23
  327.2 20.9 %collective-permute-start.61 = (bf16[640,512]{1,0:T(8,128)(2,1)}, bf16[640,512]{1,0:T(8,128)(2,1)}, u32[]{:S(2)}, u32[]{:S(2)}) collective-permute-start(bf16[640,512]{1,0:T(8,128)(2,1)} %fusion.8), channel_id=1, source_target_pairs={{0,8},{4,12},{8,0},{12,4},{16,20},{20,16},{24,28},{28,24},{1,9},{5... | collective-permute-start | bytes 1966088 | tf_op jit(solution)/shard_map/ppermute | solution.py:71
  352.4 48.0 %collective-permute-start.69 = (bf16[2,240,1280]{2,1,0:T(8,128)(2,1)}, bf16[2,240,1280]{2,1,0:T(8,128)(2,1)}, u32[]{:S(2)}, u32[]{:S(2)}) collective-permute-start(bf16[2,240,1280]{2,1,0:T(8,128)(2,1)} %copy-done.109), channel_id=1, source_target_pairs={{0,4},{4,0},{8,12},{12,8},{16,24},{20,28},{24,16},{28,20},{1,5},{5... | collective-permute-start | bytes 3686408 | tf_op jit(solution)/shard_map/ppermute | solution.py:66
  353.3 120.6 %reduce-scatter.8.cloned.1.call-start = ((), (), s32[]{:S(2)}) async-start(), calls=%async_computation.6 | async-start | bytes 1638400 | tf_op jit(solution)/shard_map/reduce_scatter | solution.py:613
  358.0 44.4 %collective-permute-start.68 = (bf16[2,640,512]{2,1,0:T(8,128)(2,1)}, bf16[2,640,512]{2,1,0:T(8,128)(2,1)}, u32[]{:S(2)}, u32[]{:S(2)}) collective-permute-start(bf16[2,640,512]{2,1,0:T(8,128)(2,1)} %get-tuple-element.290), channel_id=1, source_target_pairs={{0,4},{4,0},{8,12},{12,8},{16,24},{20,28},{24,16},{28,20},{1,5},{5... | collective-permute-start | bytes 3932168 | tf_op jit(solution)/shard_map/ppermute | solution.py:66
  372.6 32.3 %collective-permute-start.67 = (bf16[256,2560]{1,0:T(8,128)(2,1)}, bf16[256,2560]{1,0:T(8,128)(2,1)}, u32[]{:S(2)}, u32[]{:S(2)}) collective-permute-start(bf16[256,2560]{1,0:T(8,128)(2,1)} %get-tuple-element.295), channel_id=1, source_target_pairs={{0,16},{16,0},{1,17},{17,1},{2,18},{18,2},{3,19},{19,3},{4,20},{20... | collective-permute-start | bytes 3932168 | tf_op jit(solution)/shard_map/ppermute | solution.py:23
  376.0 38.5 %collective-permute-start.74 = (bf16[240,2560]{1,0:T(8,128)(2,1)}, bf16[240,2560]{1,0:T(8,128)(2,1)}, u32[]{:S(2)}, u32[]{:S(2)}) collective-permute-start(bf16[240,2560]{1,0:T(8,128)(2,1)} %fusion.5), channel_id=1, source_target_pairs={{0,8},{4,12},{8,0},{12,4},{16,20},{20,16},{24,28},{28,24},{1,9},{5... | collective-permute-start | bytes 3686408 | tf_op jit(solution)/shard_map/ppermute | solution.py:71
  412.2 16.8 %collective-permute-start.72 = (bf16[640,256]{1,0:T(8,128)(2,1)}, bf16[640,256]{1,0:T(8,128)(2,1)}, u32[]{:S(2)}, u32[]{:S(2)}) collective-permute-start(bf16[640,256]{1,0:T(8,128)(2,1)} %get-tuple-element.323), channel_id=1, source_target_pairs={{0,8},{4,12},{8,0},{12,4},{1,9},{5,13},{9,1},{13,5},{2,10},{6,14},... | collective-permute-start | bytes 983048 | tf_op jit(solution)/shard_map/ppermute | solution.py:32
  413.0 16.0 %collective-permute-start.71 = (bf16[640,256]{1,0:T(8,128)(2,1)}, bf16[640,256]{1,0:T(8,128)(2,1)}, u32[]{:S(2)}, u32[]{:S(2)}) collective-permute-start(bf16[640,256]{1,0:T(8,128)(2,1)} %get-tuple-element.322), channel_id=1, source_target_pairs={{0,12},{4,8},{8,4},{12,0},{1,13},{5,9},{9,5},{13,1},{2,14},{6,10},... | collective-permute-start | bytes 983048 | tf_op jit(solution)/shard_map/ppermute | solution.py:32
  420.1 76.5 %reduce-scatter.10.cloned.1.call-start = ((), (), s32[]{:S(2)}) async-start(), calls=%async_computation.7 | async-start | bytes 819200 | tf_op jit(solution)/shard_map/reduce_scatter | solution.py:613
  429.0 44.9 %collective-permute-start.75 = (bf16[2,240,2560]{2,1,0:T(8,128)(2,1)}, bf16[2,240,2560]{2,1,0:T(8,128)(2,1)}, u32[]{:S(2)}, u32[]{:S(2)}) collective-permute-start(bf16[2,240,2560]{2,1,0:T(8,128)(2,1)} %copy-done.108), channel_id=1, source_target_pairs={{0,4},{4,0},{8,12},{12,8},{16,24},{20,28},{24,16},{28,20},{1,5},{5... | collective-permute-start | bytes 7372808 | tf_op jit(solution)/shard_map/ppermute | solution.py:66
  440.6 16.8 %collective-permute-start.77 = (bf16[240,1280]{1,0:T(8,128)(2,1)S(1)}, bf16[240,1280]{1,0:T(8,128)(2,1)S(1)}, u32[]{:S(2)}, u32[]{:S(2)}) collective-permute-start(bf16[240,1280]{1,0:T(8,128)(2,1)S(1)} %copy-done.121), channel_id=1, source_target_pairs={{0,8},{4,12},{8,0},{12,4},{16,20},{20,16},{24,28},{28,24},{1,9},{5... | collective-permute-start | bytes 1843208 | tf_op jit(solution)/shard_map/ppermute | solution.py:71
  442.2 29.3 %collective-permute-start.76 = (bf16[640,512]{1,0:T(8,128)(2,1)}, bf16[640,512]{1,0:T(8,128)(2,1)}, u32[]{:S(2)}, u32[]{:S(2)}) collective-permute-start(bf16[640,512]{1,0:T(8,128)(2,1)} %fusion.9), channel_id=1, source_target_pairs={{0,8},{4,12},{8,0},{12,4},{16,20},{20,16},{24,28},{28,24},{1,9},{5... | collective-permute-start | bytes 1966088 | tf_op jit(solution)/shard_map/ppermute | solution.py:71
  443.6 34.9 %collective-permute-start.52 = (bf16[256,960]{1,0:T(8,128)(2,1)}, bf16[256,960]{1,0:T(8,128)(2,1)}, u32[]{:S(2)}, u32[]{:S(2)}) collective-permute-start(bf16[256,960]{1,0:T(8,128)(2,1)} %broadcast_select_fusion.2), channel_id=1, source_target_pairs={{0,16},{16,0},{1,17},{17,1},{2,18},{18,2},{3,19},{19,3},{4,20},{20... | collective-permute-start | bytes 1474568 | tf_op jit(solution)/shard_map/ppermute | solution.py:23
  449.2 45.2 %collective-permute-start.85 = (bf16[2,256,1280]{2,1,0:T(8,128)(2,1)}, bf16[2,256,1280]{2,1,0:T(8,128)(2,1)}, u32[]{:S(2)}, u32[]{:S(2)}) collective-permute-start(bf16[2,256,1280]{2,1,0:T(8,128)(2,1)} %get-tuple-element.344), channel_id=1, source_target_pairs={{0,4},{4,0},{8,12},{12,8},{16,24},{20,28},{24,16},{28,20},{1,5},{5... | collective-permute-start | bytes 3932168 | tf_op jit(solution)/shard_map/ppermute | solution.py:66
  461.7 55.2 %reduce-scatter.12.cloned.1.call-start = ((), (), s32[]{:S(2)}) async-start(), calls=%async_computation.8 | async-start | bytes 819200 | tf_op jit(solution)/shard_map/reduce_scatter | solution.py:613
  476.9 20.5 %collective-permute-start.84 = (bf16[240,2560]{1,0:T(8,128)(2,1)}, bf16[240,2560]{1,0:T(8,128)(2,1)}, u32[]{:S(2)}, u32[]{:S(2)}) collective-permute-start(bf16[240,2560]{1,0:T(8,128)(2,1)} %fusion.6), channel_id=1, source_target_pairs={{0,8},{4,12},{8,0},{12,4},{16,20},{20,16},{24,28},{28,24},{1,9},{5... | collective-permute-start | bytes 3686408 | tf_op jit(solution)/shard_map/ppermute | solution.py:71
  480.8 83.2 %reduce-scatter.14.cloned.1.call-start = ((), (), s32[]{:S(2)}) async-start(), calls=%async_computation.9 | async-start | bytes 1638400 | tf_op jit(solution)/shard_map/reduce_scatter | solution.py:613
  520.3 40.7 %collective-permute-start.89 = (bf16[76,1280]{1,0:T(8,128)(2,1)S(1)}, bf16[76,1280]{1,0:T(8,128)(2,1)}, u32[]{:S(2)}, u32[]{:S(2)}) collective-permute-start(bf16[76,1280]{1,0:T(8,128)(2,1)S(1)} %get-tuple-element.365), channel_id=1, source_target_pairs={{0,2},{1,3},{2,0},{3,1},{4,6},{5,7},{6,4},{7,5},{8,10},{9,11},{10,... | collective-permute-start | bytes 583688 | tf_op jit(solution)/shard_map/ppermute | solution.py:32
  525.3 35.7 %collective-permute-start.90 = (bf16[76,1280]{1,0:T(8,128)(2,1)S(1)}, bf16[76,1280]{1,0:T(8,128)(2,1)}, u32[]{:S(2)}, u32[]{:S(2)}) collective-permute-start(bf16[76,1280]{1,0:T(8,128)(2,1)S(1)} %get-tuple-element.367), channel_id=1, source_target_pairs={{0,1},{1,0},{2,3},{3,2},{4,5},{5,4},{6,7},{7,6},{8,9},{9,8},{10,11... | collective-permute-start | bytes 583688 | tf_op jit(solution)/shard_map/ppermute | solution.py:32
  (167 other events, 885.2 us)
Sparse Core Ops, SparseCore 0:
  13.5 45.5 all-gather.6
  77.3 45.8 all-gather.8
  150.3 41.5 all-gather.10
  353.4 31.7 reduce-scatter.5
  420.2 40.6 reduce-scatter.7
  463.6 29.3 reduce-scatter.9
  495.8 21.0 reduce-scatter.11
  519.2 41.8 reduce-scatter.13
where the time goes:
time: 587 us; the launch traced here: 578 us
  waiting for transfers between devices  191 us (33%)
  Pallas kernels  157 us (27%)
  starting transfers between devices  85.4 us (15%)
  local copies, waits for them, and re-layouts  79.4 us (14%)
  other arithmetic  48.8 us (8%)
  between operations  15.8 us (3%)
    ppermute x21, waiting for transfers between devices, across(): return lax.ppermute(array, axis, [(i, i ^ mask) for i in range(count)])  108 us
    pallas_call x14, Pallas kernels, local_call(): pl.pallas_call(kernel, out_shape=outs, in_specs=[pl.BlockSpec(memory_spac...  108 us
    unnamed x268, local copies, waits for them, and re-layouts  63.1 us
    ppermute x14, waiting for transfers between devices, second_way(): return lax.ppermute(array, ('pipe', 'ctx'), pairs)  45 us
    pallas_call x3, Pallas kernels, call(): pl.pallas_call(body, out_shape=outs, in_specs=[pl.BlockSpec(memory_space=...  45 us
    ppermute x21, starting transfers between devices, across(): return lax.ppermute(array, axis, [(i, i ^ mask) for i in range(count)])  40.9 us
    ppermute x14, starting transfers between devices, second_way(): return lax.ppermute(array, ('pipe', 'ctx'), pairs)  19.8 us
    ppermute x46, waiting for transfers between devices, swap_cores(): return lax.ppermute(array, 'pipe', [(0, 1), (1, 0)])  16.8 us
  transfers between devices with their start and end apart: 101, of which 38 were waited for; matrix products, arithmetic and copies ran while one was open for 12% of the time, Pallas kernels for 24%

commit v1 on v0

--- a/solution.py
+++ b/solution.py
@@ -602,10 +602,15 @@
             self.flights = [second_way(self.order.wait(sent.astype(BF16)))]
             return
         total = self.land()
-        if self.step == 3:
+        if self.step == 4:
             self.result = total
             return
         low = total.astype(BF16)
+        if self.step == 3:
+            sent = self.order.wait(index(low, 1 - self.high_bit, 0, False))
+            self.kept = [index(low, self.high_bit, 0, False)]
+            self.flights = [across(sent, "fsdp", 2)]
+            return
         if self.offload:
             count = lax.axis_size("fsdp")
             parts = low.reshape(count, low.shape[0] // count, low.shape[1])
@@ -626,11 +631,11 @@
         if self.extra:
             tails = jnp.broadcast_to(tail, (4, *tail.shape))
             parts = jnp.concatenate([parts, tails], axis=1)
-        here = self.zed % 4
-        self.kept = [index(parts, here, 0, False)]
-        sent = [index(parts, here ^ mask, 0, False) for mask in (3, 2, 1)]
-        sent = self.order.waits(sent)
-        self.flights = [across(block, "fsdp", mask) for block, mask in zip(sent, (3, 2, 1))]
+        low_bit, self.high_bit = self.zed % 2, self.zed % 4 // 2
+        pairs = parts.reshape(2, 2, *parts.shape[1:])
+        sent = self.order.wait(index(pairs, 1 - low_bit, 1, False))
+        self.kept = [index(pairs, low_bit, 1, False)]
+        self.flights = [across(sent, "fsdp", 1)]
 
     def settle(self):
         self.result = self.order.wait(self.result)
@@ -1095,6 +1100,7 @@
     gateup.advance()
     section_in_grad = order.wait(jnp.stack(to_layers(input_grads[0], input_grads[1])))
     attn.advance()
+    attn.advance()
     down.settle()
     down_left, down_right = order.waits(to_layers(down.result, above[0].result))
     attn.advance()

time: 587 us -> 585 us (level)
  starting transfers between devices: 85.4 us -> 92.2 us
    reduce_scatter x5, waiting for transfers between devices: 7.95 us -> 0.05 us  [advance(): lax.psum_scatter(parts, 'fsdp', scatter_dimension=0, tiled=False)]
    ppermute x21 -> x20, starting transfers between devices: 40.9 us -> 47.5 us  [across(): return lax.ppermute(array, axis, [(i, i ^ mask) for i in range(count)])]
    ppermute x21 -> x20, waiting for transfers between devices: 108 us -> 111 us  [across(): return lax.ppermute(array, axis, [(i, i ^ mask) for i in range(count)])]
    convert_element_type x6 -> x7, other arithmetic: 14.9 us -> 15 us  [advance(): low = total.astype(BF16)]
  transfers between devices with their start and end apart: 101 -> 100, of which waited for: 38 -> 37; matrix products, arithmetic and copies ran while one was open for 12% -> 11% of each run, Pallas kernels for 24% -> 24%
where the time goes in v1:
time: 585 us; the launch traced here: 576 us
  waiting for transfers between devices  186 us (32%)
  Pallas kernels  157 us (27%)
  starting transfers between devices  92.2 us (16%)
  local copies, waits for them, and re-layouts  79.5 us (14%)
  other arithmetic  45.4 us (8%)
  between operations  15.8 us (3%)
    ppermute x20, waiting for transfers between devices, across(): return lax.ppermute(array, axis, [(i, i ^ mask) for i in range(count)])  111 us
    pallas_call x14, Pallas kernels, local_call(): pl.pallas_call(kernel, out_shape=outs, in_specs=[pl.BlockSpec(memory_spac...  107 us
    unnamed x268, local copies, waits for them, and re-layouts  63.1 us
    ppermute x20, starting transfers between devices, across(): return lax.ppermute(array, axis, [(i, i ^ mask) for i in range(count)])  47.5 us
    ppermute x14, waiting for transfers between devices, second_way(): return lax.ppermute(array, ('pipe', 'ctx'), pairs)  45.1 us
    pallas_call x3, Pallas kernels, call(): pl.pallas_call(body, out_shape=outs, in_specs=[pl.BlockSpec(memory_space=...  45 us
    ppermute x14, starting transfers between devices, second_way(): return lax.ppermute(array, ('pipe', 'ctx'), pairs)  19.9 us
    ppermute x46, waiting for transfers between devices, swap_cores(): return lax.ppermute(array, 'pipe', [(0, 1), (1, 0)])  16.7 us
  transfers between devices with their start and end apart: 100, of which 37 were waited for; matrix products, arithmetic and copies ran while one was open for 11% of the time, Pallas kernels for 24%

profile of v1, /device:TPU:0, one launch (start us, length us, event | category | flops | bytes accessed | tf_op | source)
XLA Modules:
  0.0 575.7 jit_solution(17592918208869208258)
XLA Ops:
  15.3 3.0 collective-permute-start.1
  18.3 2.6 collective-permute-start.3
  20.9 4.2 collective-permute-done.1
  25.2 11.2 %collective-permute-done.3 = bf16[1,120,640]{2,1,0:T(8,128)(2,1)S(1)} collective-permute-done((bf16[1,120,640]{2,1,0:T(8,128)(2,1)S(1)}, bf16[1,120,640]{2,1,0:T(8,128)(2,1)S(1)}, u32[]{:S(2)}, u32[]{:S(2)}) %collective-permute-start.3) | collective-permute-done | bytes 153632 | tf_op jit(solution)/shard_map/ppermute | solution.py:32
  40.8 10.4 %collective-permute-start.10 = (bf16[1,240,640]{2,1,0:T(8,128)(2,1)S(1)}, bf16[1,240,640]{2,1,0:T(8,128)(2,1)S(1)}, u32[]{:S(2)}, u32[]{:S(2)}) collective-permute-start(bf16[1,240,640]{2,1,0:T(8,128)(2,1)S(1)} %bitcast.137), channel_id=1, source_target_pairs={{0,1},{1,0},{2,3},{3,2},{4,5},{5,4},{6,7},{7,6},{8,9},{9,8},{10,11... | collective-permute-start | bytes 921608 | tf_op jit(solution)/shard_map/ppermute | solution.py:32
  51.3 2.3 collective-permute-start.9
  56.4 9.1 %collective-permute-done.10 = bf16[1,240,640]{2,1,0:T(8,128)(2,1)S(1)} collective-permute-done((bf16[1,240,640]{2,1,0:T(8,128)(2,1)S(1)}, bf16[1,240,640]{2,1,0:T(8,128)(2,1)S(1)}, u32[]{:S(2)}, u32[]{:S(2)}) %collective-permute-start.10) | collective-permute-done | bytes 307232 | tf_op jit(solution)/shard_map/ppermute | solution.py:32
  65.5 11.5 %collective-permute-done.9 = bf16[1,240,640]{2,1,0:T(8,128)(2,1)S(1)} collective-permute-done((bf16[1,240,640]{2,1,0:T(8,128)(2,1)S(1)}, bf16[1,240,640]{2,1,0:T(8,128)(2,1)S(1)}, u32[]{:S(2)}, u32[]{:S(2)}) %collective-permute-start.9) | collective-permute-done | bytes 307232 | tf_op jit(solution)/shard_map/ppermute | solution.py:32
  81.9 2.0 constant_dynamic-slice_fusion
  85.0 2.8 shard_map.169
  87.8 2.2 copy-done
  90.0 3.7 shard_map.170
  95.8 2.2 collective-permute-start.18
  98.8 14.8 %collective-permute-done.16.p1 = bf16[640,256]{1,0:T(8,128)(2,1)S(1)} collective-permute-done((bf16[640,256]{1,0:T(8,128)(2,1)S(1)}, bf16[640,256]{1,0:T(8,128)(2,1)S(1)}, u32[]{:S(2)}, u32[]{:S(2)}) %collective-permute-start.16) | collective-permute-done | bytes 327712 | tf_op jit(solution)/shard_map/ppermute | solution.py:32
  117.8 3.4 collective-permute-start.22
  126.6 12.1 %shard_map.171 = (bf16[960,256]{1,0:T(8,128)(2,1)S(1)}, bf16[960,256]{1,0:T(8,128)(2,1)S(1)}, f32[15,1,256]{2,1,0:T(1,128)S(1)}, f32[256,960]{1,0:T(8,128)S(1)}, bf16[960,256]{1,0:T(8,128)(2,1)}) custom-call(bf16[960,256]{1,0:T(8,128)(2,1)S(1)} %copy-done.40, bf16[640,256]{1,0:T(8,128)(2,1)S(1)} %copy-done.46, bf16[640,256]{1,0:T(8,128)(2,1)S(1)} %copy-done.49, ...), custom_call_target="tpu_custom_call" | custom-call | tf_op jit(solution)/shard_map/pallas_call | solution.py:656
  141.3 3.0 collective-permute-done.22.refs_3_
  152.5 12.0 %shard_map.172 = (bf16[256,960]{1,0:T(8,128)(2,1)S(1)}, bf16[960,256]{1,0:T(8,128)(2,1)S(1)}, f32[256,2560]{1,0:T(8,128)}, f32[256,2560]{1,0:T(8,128)}, bf16[2560,256]{1,0:T(8,128)(2,1)}) custom-call(f32[256,960]{1,0:T(8,128)S(1)} %copy-done.6, f32[1,960]{1,0:T(1,128)S(1)} %get-tuple-element.422.gain_ref, bf16[4,240,640]{2,1,0:T(8,128)(2,1)S(1)} %pad_maximum_fusion.refs_0_, ...), custom_call_target="tpu_custom_call" | custom-call | tf_op jit(solution)/shard_map/pallas_call | solution.py:294
  164.5 2.2 collective-permute-start.32
  168.7 12.5 %collective-permute-done.32.refs_3_ = bf16[4,120,640]{2,1,0:T(8,128)(2,1)S(1)} collective-permute-done((bf16[4,120,640]{2,1,0:T(8,128)(2,1)}, bf16[4,120,640]{2,1,0:T(8,128)(2,1)S(1)}, u32[]{:S(2)}, u32[]{:S(2)}) %collective-permute-start.32) | collective-permute-done | bytes 614432 | tf_op jit(solution)/shard_map/ppermute | solution.py:71
  181.8 2.5 collective-permute-done.34.refs_5_
  186.2 2.3 copy-done.1
  188.5 3.7 shard_map.174
  194.8 2.2 collective-permute-start.40
  198.4 6.6 %collective-permute-done.38.refs_2_ = bf16[4,240,640]{2,1,0:T(8,128)(2,1)} collective-permute-done((bf16[4,240,640]{2,1,0:T(8,128)(2,1)S(1)}, bf16[4,240,640]{2,1,0:T(8,128)(2,1)}, u32[]{:S(2)}, u32[]{:S(2)}) %collective-permute-start.38) | collective-permute-done | bytes 1228832 | tf_op jit(solution)/shard_map/ppermute | solution.py:71
  205.0 2.8 collective-permute-start.42
  208.5 6.3 %collective-permute-done.40.p2 = bf16[640,256]{1,0:T(8,128)(2,1)S(1)} collective-permute-done((bf16[640,256]{1,0:T(8,128)(2,1)S(1)}, bf16[640,256]{1,0:T(8,128)(2,1)S(1)}, u32[]{:S(2)}, u32[]{:S(2)}) %collective-permute-start.40) | collective-permute-done | bytes 327712 | tf_op jit(solution)/shard_map/ppermute | solution.py:32
  223.9 12.4 %shard_map.175 = (bf16[960,256]{1,0:T(8,128)(2,1)S(1)}, bf16[960,256]{1,0:T(8,128)(2,1)}, f32[15,1,256]{2,1,0:T(1,128)S(1)}, f32[256,960]{1,0:T(8,128)S(1)}, bf16[960,256]{1,0:T(8,128)(2,1)}) custom-call(bf16[960,256]{1,0:T(8,128)(2,1)S(1)} %copy-done.43, bf16[640,256]{1,0:T(8,128)(2,1)S(1)} %copy-done.58, bf16[640,256]{1,0:T(8,128)(2,1)S(1)} %copy-done.61, ...), custom_call_target="tpu_custom_call" | custom-call | tf_op jit(solution)/shard_map/pallas_call | solution.py:656
  243.6 2.0 copy.38
  252.3 19.6 %shard_map.176 = (bf16[256,960]{1,0:T(8,128)(2,1)S(1)}, bf16[960,256]{1,0:T(8,128)(2,1)S(1)}, bf16[2560,256]{1,0:T(8,128)(2,1)}, f32[256,960]{1,0:T(8,128)S(1)},...) custom-call(f32[256,960]{1,0:T(8,128)S(1)} %copy-done.82, ...), custom_call_target="tpu_custom_call" | custom-call | tf_op jit(solution)/shard_map/pallas_call | solution.py:294
  273.9 3.9 collective-permute-done.54.refs_3_
  282.4 21.2 %shard_map.178 = (bf16[960,256]{1,0:T(8,128)(2,1)S(1)}, bf16[960,256]{1,0:T(8,128)(2,1)}, f32[640,256]{1,0:T(8,128)}, bf16[640,256]{1,0:T(8,128)(2,1)S(1)}, bf16...) custom-call(f32[256,960]{1,0:T(8,128)} %copy-done.8, ...), custom_call_target="tpu_custom_call" | custom-call | tf_op jit(solution)/shard_map/pallas_call | solution.py:656
  305.4 2.5 collective-permute-start.58
  308.3 5.4 shard_map.179
  315.4 6.4 %collective-permute-done.58.kv2 = bf16[640,256]{1,0:T(8,128)(2,1)S(1)} collective-permute-done((bf16[640,256]{1,0:T(8,128)(2,1)S(1)}, bf16[640,256]{1,0:T(8,128)(2,1)S(1)}, u32[]{:S(2)}, u32[]{:S(2)}) %collective-permute-start.58) | collective-permute-done | bytes 327712 | tf_op jit(solution)/shard_map/ppermute | solution.py:32
  324.9 2.4 fusion.9
  333.4 4.1 shard_map.180
  344.7 3.4 shard_map.181
  348.2 3.2 fusion.4
  354.0 4.1 shard_map.182
  359.1 13.4 %shard_map.183 = (f32[256,960]{1,0:T(8,128)S(1)}, f32[1,960]{1,0:T(1,128)S(1)}, bf16[256,2560]{1,0:T(8,128)(2,1)}, bf16[256,2560]{1,0:T(8,128)(2,1)}) custom-call(bf16[256,960]{1,0:T(8,128)(2,1)S(1)} %get-tuple-element.289.grad_ref, f32[256,960]{1,0:T(8,128)S(1)} %copy-done.7, f32[1,960]{1,0:T(1,128)S(1)} %get-tuple-element.422.gain_ref, ...), custom_call_target="tpu_custom_call" | custom-call | tf_op jit(solution)/shard_map/pallas_call | solution.py:294
  372.9 3.2 fusion.5
  377.1 21.7 %shard_map.185 = (bf16[960,256]{1,0:T(8,128)(2,1)S(1)}, bf16[960,256]{1,0:T(8,128)(2,1)S(1)}, f32[640,256]{1,0:T(8,128)}, bf16[640,256]{1,0:T(8,128)(2,1)}, bf16...) custom-call(f32[256,960]{1,0:T(8,128)} %copy-done.10, ...), custom_call_target="tpu_custom_call" | custom-call | tf_op jit(solution)/shard_map/pallas_call | solution.py:656
  400.4 2.1 fusion.13
  402.5 2.4 fusion.10
  405.0 6.1 %shard_map.184 = (bf16[2,240,2560]{2,1,0:T(8,128)(2,1)S(1)}, bf16[2,240,2560]{2,1,0:T(8,128)(2,1)}) custom-call(bf16[960,256]{1,0:T(8,128)(2,1)S(1)} %copy-done.86, bf16[960,256]{1,0:T(8,128)(2,1)S(1)} %copy-done.88, bf16[256,2560]{1,0:T(8,128)(2,1)S(1)} %copy-done.70, bf16[256,2560]{1,0:T(8,128)(2,1)} %collective-permute-done.67.refs_3_), custom_call_target="tpu_custom_call" | custom-call | tf_op jit(solution)/shard_map/pallas_call | solution.py:656
  414.6 3.1 fusion.1
  417.7 2.3 reshape.124
  422.6 6.4 %collective-permute-done.72.kv2 = bf16[640,256]{1,0:T(8,128)(2,1)} collective-permute-done((bf16[640,256]{1,0:T(8,128)(2,1)}, bf16[640,256]{1,0:T(8,128)(2,1)}, u32[]{:S(2)}, u32[]{:S(2)}) %collective-permute-start.72) | collective-permute-done | bytes 327712 | tf_op jit(solution)/shard_map/ppermute | solution.py:32
  434.0 4.5 shard_map.186
  445.0 3.1 shard_map.187
  450.3 7.1 %collective-permute-done.77 = bf16[240,1280]{1,0:T(8,128)(2,1)S(1)} collective-permute-done((bf16[240,1280]{1,0:T(8,128)(2,1)S(1)}, bf16[240,1280]{1,0:T(8,128)(2,1)S(1)}, u32[]{:S(2)}, u32[]{:S(2)}) %collective-permute-start.77) | collective-permute-done | bytes 614432 | tf_op jit(solution)/shard_map/ppermute | solution.py:71
  457.4 2.1 fusion.7
  459.5 2.1 reshape.125
  461.7 9.8 %collective-permute-done.76 = bf16[640,512]{1,0:T(8,128)(2,1)} collective-permute-done((bf16[640,512]{1,0:T(8,128)(2,1)}, bf16[640,512]{1,0:T(8,128)(2,1)}, u32[]{:S(2)}, u32[]{:S(2)}) %collective-permute-start.76) | collective-permute-done | bytes 655392 | tf_op jit(solution)/shard_map/ppermute | solution.py:71
  471.6 2.4 fusion.3
  474.0 3.0 fusion.6
  483.1 11.3 %collective-permute-done.85 = bf16[2,256,1280]{2,1,0:T(8,128)(2,1)} collective-permute-done((bf16[2,256,1280]{2,1,0:T(8,128)(2,1)}, bf16[2,256,1280]{2,1,0:T(8,128)(2,1)}, u32[]{:S(2)}, u32[]{:S(2)}) %collective-permute-start.85) | collective-permute-done | bytes 1310752 | tf_op jit(solution)/shard_map/ppermute | solution.py:66
  497.5 2.5 fusion
  501.5 5.0 collective-permute-done.86
  508.2 11.5 %collective-permute-start.87 = (bf16[2,76,1280]{2,1,0:T(8,128)(2,1)S(1)}, bf16[2,76,1280]{2,1,0:T(8,128)(2,1)S(1)}, u32[]{:S(2)}, u32[]{:S(2)}) collective-permute-start(bf16[2,76,1280]{2,1,0:T(8,128)(2,1)S(1)} %fusion.15), channel_id=1, source_target_pairs={{0,1},{1,0},{2,3},{3,2},{4,5},{5,4},{6,7},{7,6},{8,9},{9,8},{10,11... | collective-permute-start | bytes 1167368 | tf_op jit(solution)/shard_map/ppermute | solution.py:32
  519.8 14.5 %collective-permute-done.87 = bf16[2,76,1280]{2,1,0:T(8,128)(2,1)S(1)} collective-permute-done((bf16[2,76,1280]{2,1,0:T(8,128)(2,1)S(1)}, bf16[2,76,1280]{2,1,0:T(8,128)(2,1)S(1)}, u32[]{:S(2)}, u32[]{:S(2)}) %collective-permute-start.87) | collective-permute-done | bytes 389152 | tf_op jit(solution)/shard_map/ppermute | solution.py:32
  539.8 20.2 %collective-permute-done.88 = bf16[76,1280]{1,0:T(8,128)(2,1)S(1)} collective-permute-done((bf16[76,1280]{1,0:T(8,128)(2,1)S(1)}, bf16[76,1280]{1,0:T(8,128)(2,1)S(1)}, u32[]{:S(2)}, u32[]{:S(2)}) %collective-permute-start.88) | collective-permute-done | bytes 194592 | tf_op jit(solution)/shard_map/ppermute | solution.py:32
  566.2 2.3 copy.45
  (516 shorter events, 153.2 us)
Async XLA Ops:
  7.2 114.0 %all-gather.7.cloned.1.call-start = ((), (), s32[]{:S(2)}) async-start(), calls=%async_computation.10 | async-start | bytes 1638400 | tf_op jit(solution)/shard_map/all_gather | solution.py:232
  13.4 127.9 %all-gather.9.cloned.1.call-start = ((), (), s32[]{:S(2)}) async-start(), calls=%async_computation.11 | async-start | bytes 2304000 | tf_op jit(solution)/shard_map/all_gather | solution.py:963
  18.3 18.0 %collective-permute-start.3 = (bf16[1,120,640]{2,1,0:T(8,128)(2,1)S(1)}, bf16[1,120,640]{2,1,0:T(8,128)(2,1)S(1)}, u32[]{:S(2)}, u32[]{:S(2)}) collective-permute-start(bf16[1,120,640]{2,1,0:T(8,128)(2,1)S(1)} %get-tuple-element.415), channel_id=1, source_target_pairs={{0,2},{1,3},{2,0},{3,1},{4,6},{5,7},{6,4},{7,5},{8,10},{9,11},{10,... | collective-permute-start | bytes 460808 | tf_op jit(solution)/shard_map/ppermute | solution.py:32
  20.9 15.4 %collective-permute-start.4 = (bf16[1,120,640]{2,1,0:T(8,128)(2,1)S(1)}, bf16[1,120,640]{2,1,0:T(8,128)(2,1)S(1)}, u32[]{:S(2)}, u32[]{:S(2)}) collective-permute-start(bf16[1,120,640]{2,1,0:T(8,128)(2,1)S(1)} %get-tuple-element.415), channel_id=1, source_target_pairs={{0,3},{1,2},{2,1},{3,0},{4,7},{5,6},{6,5},{7,4},{8,11},{9,10},{10,... | collective-permute-start | bytes 460808 | tf_op jit(solution)/shard_map/ppermute | solution.py:32
  37.3 17.7 %collective-permute-start.5 = (bf16[4,120,640]{2,1,0:T(8,128)(2,1)}, bf16[4,120,640]{2,1,0:T(8,128)(2,1)}, u32[]{:S(2)}, u32[]{:S(2)}) collective-permute-start(bf16[4,120,640]{2,1,0:T(8,128)(2,1)} %pad_maximum_fusion.3.refs_0_), channel_id=1, source_target_pairs={{0,4},{4,0},{8,12},{12,8},{16,24},{20,28},{24,16},{28,20},{1,5},{5... | collective-permute-start | bytes 1843208 | tf_op jit(solution)/shard_map/ppermute | solution.py:66
  38.8 16.2 %collective-permute-start.6 = (bf16[4,120,640]{2,1,0:T(8,128)(2,1)}, bf16[4,120,640]{2,1,0:T(8,128)(2,1)}, u32[]{:S(2)}, u32[]{:S(2)}) collective-permute-start(bf16[4,120,640]{2,1,0:T(8,128)(2,1)} %pad_maximum_fusion.3.refs_0_), channel_id=1, source_target_pairs={{0,8},{4,12},{8,0},{12,4},{16,20},{20,16},{24,28},{28,24},{1,9},{5... | collective-permute-start | bytes 1843208 | tf_op jit(solution)/shard_map/ppermute | solution.py:71
  40.8 24.7 %collective-permute-start.10 = (bf16[1,240,640]{2,1,0:T(8,128)(2,1)S(1)}, bf16[1,240,640]{2,1,0:T(8,128)(2,1)S(1)}, u32[]{:S(2)}, u32[]{:S(2)}) collective-permute-start(bf16[1,240,640]{2,1,0:T(8,128)(2,1)S(1)} %bitcast.137), channel_id=1, source_target_pairs={{0,1},{1,0},{2,3},{3,2},{4,5},{5,4},{6,7},{7,6},{8,9},{9,8},{10,11... | collective-permute-start | bytes 921608 | tf_op jit(solution)/shard_map/ppermute | solution.py:32
  51.3 25.8 %collective-permute-start.9 = (bf16[1,240,640]{2,1,0:T(8,128)(2,1)S(1)}, bf16[1,240,640]{2,1,0:T(8,128)(2,1)S(1)}, u32[]{:S(2)}, u32[]{:S(2)}) collective-permute-start(bf16[1,240,640]{2,1,0:T(8,128)(2,1)S(1)} %bitcast.138), channel_id=1, source_target_pairs={{0,2},{1,3},{2,0},{3,1},{4,6},{5,7},{6,4},{7,5},{8,10},{9,11},{10,... | collective-permute-start | bytes 921608 | tf_op jit(solution)/shard_map/ppermute | solution.py:32
  53.6 23.5 %collective-permute-start.8 = (bf16[1,240,640]{2,1,0:T(8,128)(2,1)S(1)}, bf16[1,240,640]{2,1,0:T(8,128)(2,1)S(1)}, u32[]{:S(2)}, u32[]{:S(2)}) collective-permute-start(bf16[1,240,640]{2,1,0:T(8,128)(2,1)S(1)} %bitcast.139), channel_id=1, source_target_pairs={{0,3},{1,2},{2,1},{3,0},{4,7},{5,6},{6,5},{7,4},{8,11},{9,10},{10,... | collective-permute-start | bytes 921608 | tf_op jit(solution)/shard_map/ppermute | solution.py:32
  55.0 26.4 %collective-permute-start.11 = (bf16[4,120,640]{2,1,0:T(8,128)(2,1)}, bf16[4,120,640]{2,1,0:T(8,128)(2,1)}, u32[]{:S(2)}, u32[]{:S(2)}) collective-permute-start(bf16[4,120,640]{2,1,0:T(8,128)(2,1)} %pad_maximum_fusion.3.refs_0_), channel_id=1, source_target_pairs={{0,16},{16,0},{1,17},{17,1},{2,18},{18,2},{3,19},{19,3},{4,20},{20... | collective-permute-start | bytes 1843208 | tf_op jit(solution)/shard_map/ppermute | solution.py:23
  55.0 25.8 %collective-permute-start.7 = (bf16[4,120,640]{2,1,0:T(8,128)(2,1)}, bf16[4,120,640]{2,1,0:T(8,128)(2,1)}, u32[]{:S(2)}, u32[]{:S(2)}) collective-permute-start(bf16[4,120,640]{2,1,0:T(8,128)(2,1)} %collective-permute-done.5.refs_1_), channel_id=1, source_target_pairs={{0,8},{4,12},{8,0},{12,4},{16,20},{20,16},{24,28},{28,24},{1,9},{5... | collective-permute-start | bytes 1843208 | tf_op jit(solution)/shard_map/ppermute | solution.py:71
  65.5 15.3 %collective-permute-start.15 = (f32[2,960]{1,0:T(2,128)S(1)}, f32[2,960]{1,0:T(2,128)S(1)}, u32[]{:S(2)}, u32[]{:S(2)}) collective-permute-start(f32[2,960]{1,0:T(2,128)S(1)} %pad_maximum_fusion.8), channel_id=1, source_target_pairs={{0,16},{16,0},{1,17},{17,1},{2,18},{18,2},{3,19},{19,3},{4,20},{20... | collective-permute-start | bytes 23048 | tf_op jit(solution)/shard_map/ppermute | solution.py:23
  77.1 139.2 %all-gather.11.cloned.1.call-start = ((), (), s32[]{:S(2)}) async-start(), calls=%async_computation.12 | async-start | bytes 1638400 | tf_op jit(solution)/shard_map/all_gather | solution.py:232
  77.5 40.3 %collective-permute-start.21 = (bf16[4,240,640]{2,1,0:T(8,128)(2,1)S(1)}, bf16[4,240,640]{2,1,0:T(8,128)(2,1)S(1)}, u32[]{:S(2)}, u32[]{:S(2)}) collective-permute-start(bf16[4,240,640]{2,1,0:T(8,128)(2,1)S(1)} %pad_maximum_fusion.refs_0_), channel_id=1, source_target_pairs={{0,4},{4,0},{8,12},{12,8},{16,24},{20,28},{24,16},{28,20},{1,5},{5... | collective-permute-start | bytes 3686408 | tf_op jit(solution)/shard_map/ppermute | solution.py:66
  79.3 41.9 %collective-permute-start.20 = (bf16[4,240,640]{2,1,0:T(8,128)(2,1)S(1)}, bf16[4,240,640]{2,1,0:T(8,128)(2,1)}, u32[]{:S(2)}, u32[]{:S(2)}) collective-permute-start(bf16[4,240,640]{2,1,0:T(8,128)(2,1)S(1)} %pad_maximum_fusion.refs_0_), channel_id=1, source_target_pairs={{0,8},{4,12},{8,0},{12,4},{16,20},{20,16},{24,28},{28,24},{1,9},{5... | collective-permute-start | bytes 3686408 | tf_op jit(solution)/shard_map/ppermute | solution.py:71
  94.5 19.0 %collective-permute-start.16 = (bf16[640,256]{1,0:T(8,128)(2,1)S(1)}, bf16[640,256]{1,0:T(8,128)(2,1)S(1)}, u32[]{:S(2)}, u32[]{:S(2)}) collective-permute-start(bf16[640,256]{1,0:T(8,128)(2,1)S(1)} %get-tuple-element.202.p0), channel_id=1, source_target_pairs={{0,4},{4,0},{8,12},{12,8},{1,5},{5,1},{9,13},{13,9},{2,6},{6,2},{1... | collective-permute-start | bytes 983048 | tf_op jit(solution)/shard_map/ppermute | solution.py:32
  95.4 18.9 %collective-permute-start.17 = (bf16[640,256]{1,0:T(8,128)(2,1)S(1)}, bf16[640,256]{1,0:T(8,128)(2,1)S(1)}, u32[]{:S(2)}, u32[]{:S(2)}) collective-permute-start(bf16[640,256]{1,0:T(8,128)(2,1)S(1)} %get-tuple-element.202.p0), channel_id=1, source_target_pairs={{0,8},{4,12},{8,0},{12,4},{1,9},{5,13},{9,1},{13,5},{2,10},{6,14},... | collective-permute-start | bytes 983048 | tf_op jit(solution)/shard_map/ppermute | solution.py:32
  95.8 21.2 %collective-permute-start.18 = (bf16[640,256]{1,0:T(8,128)(2,1)S(1)}, bf16[640,256]{1,0:T(8,128)(2,1)S(1)}, u32[]{:S(2)}, u32[]{:S(2)}) collective-permute-start(bf16[640,256]{1,0:T(8,128)(2,1)S(1)} %get-tuple-element.202.p0), channel_id=1, source_target_pairs={{0,12},{4,8},{8,4},{12,0},{1,13},{5,9},{9,5},{13,1},{2,14},{6,10},... | collective-permute-start | bytes 983048 | tf_op jit(solution)/shard_map/ppermute | solution.py:32
  117.8 26.6 %collective-permute-start.22 = (bf16[4,240,640]{2,1,0:T(8,128)(2,1)S(1)}, bf16[4,240,640]{2,1,0:T(8,128)(2,1)}, u32[]{:S(2)}, u32[]{:S(2)}) collective-permute-start(bf16[4,240,640]{2,1,0:T(8,128)(2,1)S(1)} %collective-permute-done.21.refs_1_), channel_id=1, source_target_pairs={{0,8},{4,12},{8,0},{12,4},{16,20},{20,16},{24,28},{28,24},{1,9},{5... | collective-permute-start | bytes 3686408 | tf_op jit(solution)/shard_map/ppermute | solution.py:71
  121.1 23.3 %collective-permute-start.27 = (bf16[4,160,960]{2,1,0:T(8,128)(2,1)}, bf16[4,160,960]{2,1,0:T(8,128)(2,1)}, u32[]{:S(2)}, u32[]{:S(2)}) collective-permute-start(bf16[4,160,960]{2,1,0:T(8,128)(2,1)} %bitcast.123), channel_id=1, source_target_pairs={{0,4},{4,0},{8,12},{12,8},{16,24},{20,28},{24,16},{28,20},{1,5},{5... | collective-permute-start | bytes 3686408 | tf_op jit(solution)/shard_map/ppermute | solution.py:66
  121.6 23.3 %collective-permute-start.23 = (bf16[4,240,640]{2,1,0:T(8,128)(2,1)S(1)}, bf16[4,240,640]{2,1,0:T(8,128)(2,1)}, u32[]{:S(2)}, u32[]{:S(2)}) collective-permute-start(bf16[4,240,640]{2,1,0:T(8,128)(2,1)S(1)} %pad_maximum_fusion.refs_0_), channel_id=1, source_target_pairs={{0,16},{16,0},{1,17},{17,1},{2,18},{18,2},{3,19},{19,3},{4,20},{20... | collective-permute-start | bytes 3686408 | tf_op jit(solution)/shard_map/ppermute | solution.py:23
  121.6 25.3 %collective-permute-start.28 = (bf16[4,160,960]{2,1,0:T(8,128)(2,1)}, bf16[4,160,960]{2,1,0:T(8,128)(2,1)}, u32[]{:S(2)}, u32[]{:S(2)}) collective-permute-start(bf16[4,160,960]{2,1,0:T(8,128)(2,1)} %bitcast.124), channel_id=1, source_target_pairs={{0,16},{16,0},{1,17},{17,1},{2,18},{18,2},{3,19},{19,3},{4,20},{20... | collective-permute-start | bytes 3686408 | tf_op jit(solution)/shard_map/ppermute | solution.py:23
  122.2 26.5 %collective-permute-start.25 = (bf16[4,240,640]{2,1,0:T(8,128)(2,1)}, bf16[4,240,640]{2,1,0:T(8,128)(2,1)}, u32[]{:S(2)}, u32[]{:S(2)}) collective-permute-start(bf16[4,240,640]{2,1,0:T(8,128)(2,1)} %collective-permute-done.20.refs_2_), channel_id=1, source_target_pairs={{0,16},{16,0},{1,17},{17,1},{2,18},{18,2},{3,19},{19,3},{4,20},{20... | collective-permute-start | bytes 3686408 | tf_op jit(solution)/shard_map/ppermute | solution.py:23
  146.9 17.6 %collective-permute-start.30 = (bf16[4,120,640]{2,1,0:T(8,128)(2,1)}, bf16[4,120,640]{2,1,0:T(8,128)(2,1)}, u32[]{:S(2)}, u32[]{:S(2)}) collective-permute-start(bf16[4,120,640]{2,1,0:T(8,128)(2,1)} %slice.104.refs_0_), channel_id=1, source_target_pairs={{0,4},{4,0},{8,12},{12,8},{16,24},{20,28},{24,16},{28,20},{1,5},{5... | collective-permute-start | bytes 1843208 | tf_op jit(solution)/shard_map/ppermute | solution.py:66
  148.7 18.1 %collective-permute-start.31 = (bf16[4,120,640]{2,1,0:T(8,128)(2,1)}, bf16[4,120,640]{2,1,0:T(8,128)(2,1)}, u32[]{:S(2)}, u32[]{:S(2)}) collective-permute-start(bf16[4,120,640]{2,1,0:T(8,128)(2,1)} %slice.104.refs_0_), channel_id=1, source_target_pairs={{0,8},{4,12},{8,0},{12,4},{16,20},{20,16},{24,28},{28,24},{1,9},{5... | collective-permute-start | bytes 1843208 | tf_op jit(solution)/shard_map/ppermute | solution.py:71
  150.1 252.4 %reduce-scatter.6.cloned.1.call-start = ((), (), s32[]{:S(2)}) async-start(), calls=%async_computation.5 | async-start | bytes 819200 | tf_op jit(solution)/shard_map/reduce_scatter | solution.py:618
  164.5 16.8 %collective-permute-start.32 = (bf16[4,120,640]{2,1,0:T(8,128)(2,1)}, bf16[4,120,640]{2,1,0:T(8,128)(2,1)S(1)}, u32[]{:S(2)}, u32[]{:S(2)}) collective-permute-start(bf16[4,120,640]{2,1,0:T(8,128)(2,1)} %collective-permute-done.30.refs_1_), channel_id=1, source_target_pairs={{0,8},{4,12},{8,0},{12,4},{16,20},{20,16},{24,28},{28,24},{1,9},{5... | collective-permute-start | bytes 1843208 | tf_op jit(solution)/shard_map/ppermute | solution.py:71
  166.7 14.6 %collective-permute-start.33 = (bf16[4,120,640]{2,1,0:T(8,128)(2,1)}, bf16[4,120,640]{2,1,0:T(8,128)(2,1)S(1)}, u32[]{:S(2)}, u32[]{:S(2)}) collective-permute-start(bf16[4,120,640]{2,1,0:T(8,128)(2,1)} %slice.104.refs_0_), channel_id=1, source_target_pairs={{0,16},{16,0},{1,17},{17,1},{2,18},{18,2},{3,19},{19,3},{4,20},{20... | collective-permute-start | bytes 1843208 | tf_op jit(solution)/shard_map/ppermute | solution.py:23
  166.8 31.6 %collective-permute-start.39 = (bf16[4,240,640]{2,1,0:T(8,128)(2,1)S(1)}, bf16[4,240,640]{2,1,0:T(8,128)(2,1)}, u32[]{:S(2)}, u32[]{:S(2)}) collective-permute-start(bf16[4,240,640]{2,1,0:T(8,128)(2,1)S(1)} %slice.106.refs_0_), channel_id=1, source_target_pairs={{0,4},{4,0},{8,12},{12,8},{16,24},{20,28},{24,16},{28,20},{1,5},{5... | collective-permute-start | bytes 3686408 | tf_op jit(solution)/shard_map/ppermute | solution.py:66
  167.9 37.1 %collective-permute-start.38 = (bf16[4,240,640]{2,1,0:T(8,128)(2,1)S(1)}, bf16[4,240,640]{2,1,0:T(8,128)(2,1)}, u32[]{:S(2)}, u32[]{:S(2)}) collective-permute-start(bf16[4,240,640]{2,1,0:T(8,128)(2,1)S(1)} %slice.106.refs_0_), channel_id=1, source_target_pairs={{0,8},{4,12},{8,0},{12,4},{16,20},{20,16},{24,28},{28,24},{1,9},{5... | collective-permute-start | bytes 3686408 | tf_op jit(solution)/shard_map/ppermute | solution.py:71
  193.8 14.0 %collective-permute-start.37 = (bf16[640,256]{1,0:T(8,128)(2,1)S(1)}, bf16[640,256]{1,0:T(8,128)(2,1)S(1)}, u32[]{:S(2)}, u32[]{:S(2)}) collective-permute-start(bf16[640,256]{1,0:T(8,128)(2,1)S(1)} %get-tuple-element.226.p0), channel_id=1, source_target_pairs={{0,4},{4,0},{8,12},{12,8},{1,5},{5,1},{9,13},{13,9},{2,6},{6,2},{1... | collective-permute-start | bytes 983048 | tf_op jit(solution)/shard_map/ppermute | solution.py:32
  194.8 20.0 %collective-permute-start.40 = (bf16[640,256]{1,0:T(8,128)(2,1)S(1)}, bf16[640,256]{1,0:T(8,128)(2,1)S(1)}, u32[]{:S(2)}, u32[]{:S(2)}) collective-permute-start(bf16[640,256]{1,0:T(8,128)(2,1)S(1)} %get-tuple-element.226.p0), channel_id=1, source_target_pairs={{0,8},{4,12},{8,0},{12,4},{1,9},{5,13},{9,1},{13,5},{2,10},{6,14},... | collective-permute-start | bytes 983048 | tf_op jit(solution)/shard_map/ppermute | solution.py:32
  197.1 18.5 %collective-permute-start.41 = (bf16[640,256]{1,0:T(8,128)(2,1)S(1)}, bf16[640,256]{1,0:T(8,128)(2,1)S(1)}, u32[]{:S(2)}, u32[]{:S(2)}) collective-permute-start(bf16[640,256]{1,0:T(8,128)(2,1)S(1)} %get-tuple-element.226.p0), channel_id=1, source_target_pairs={{0,12},{4,8},{8,4},{12,0},{1,13},{5,9},{9,5},{13,1},{2,14},{6,10},... | collective-permute-start | bytes 983048 | tf_op jit(solution)/shard_map/ppermute | solution.py:32
  198.4 41.1 %collective-permute-start.43 = (bf16[2560,256]{1,0:T(8,128)(2,1)}, bf16[2560,256]{1,0:T(8,128)(2,1)}, u32[]{:S(2)}, u32[]{:S(2)}) collective-permute-start(bf16[2560,256]{1,0:T(8,128)(2,1)} %get-tuple-element.238.refs_0_), channel_id=1, source_target_pairs={{0,16},{16,0},{1,17},{17,1},{2,18},{18,2},{3,19},{19,3},{4,20},{20... | collective-permute-start | bytes 3932168 | tf_op jit(solution)/shard_map/ppermute | solution.py:23
  205.0 35.0 %collective-permute-start.42 = (bf16[4,240,640]{2,1,0:T(8,128)(2,1)}, bf16[4,240,640]{2,1,0:T(8,128)(2,1)}, u32[]{:S(2)}, u32[]{:S(2)}) collective-permute-start(bf16[4,240,640]{2,1,0:T(8,128)(2,1)} %collective-permute-done.39.refs_1_), channel_id=1, source_target_pairs={{0,8},{4,12},{8,0},{12,4},{16,20},{20,16},{24,28},{28,24},{1,9},{5... | collective-permute-start | bytes 3686408 | tf_op jit(solution)/shard_map/ppermute | solution.py:71
  216.3 25.5 %collective-permute-start.49 = (bf16[4,160,960]{2,1,0:T(8,128)(2,1)}, bf16[4,160,960]{2,1,0:T(8,128)(2,1)}, u32[]{:S(2)}, u32[]{:S(2)}) collective-permute-start(bf16[4,160,960]{2,1,0:T(8,128)(2,1)} %bitcast.19.refs_8_), channel_id=1, source_target_pairs={{0,4},{4,0},{8,12},{12,8},{16,24},{20,28},{24,16},{28,20},{1,5},{5... | collective-permute-start | bytes 3686408 | tf_op jit(solution)/shard_map/ppermute | solution.py:66
  217.4 25.1 %collective-permute-start.45 = (bf16[4,240,640]{2,1,0:T(8,128)(2,1)S(1)}, bf16[4,240,640]{2,1,0:T(8,128)(2,1)S(1)}, u32[]{:S(2)}, u32[]{:S(2)}) collective-permute-start(bf16[4,240,640]{2,1,0:T(8,128)(2,1)S(1)} %slice.106.refs_0_), channel_id=1, source_target_pairs={{0,16},{16,0},{1,17},{17,1},{2,18},{18,2},{3,19},{19,3},{4,20},{20... | collective-permute-start | bytes 3686408 | tf_op jit(solution)/shard_map/ppermute | solution.py:23
  217.5 21.3 %collective-permute-start.44 = (bf16[960,256]{1,0:T(8,128)(2,1)}, bf16[960,256]{1,0:T(8,128)(2,1)S(1)}, u32[]{:S(2)}, u32[]{:S(2)}) collective-permute-start(bf16[960,256]{1,0:T(8,128)(2,1)} %copy-done.85), channel_id=1, source_target_pairs={{0,16},{16,0},{1,17},{17,1},{2,18},{18,2},{3,19},{19,3},{4,20},{20... | collective-permute-start | bytes 1474568 | tf_op jit(solution)/shard_map/ppermute | solution.py:23
  272.8 35.5 %collective-permute-start.57 = (bf16[256,2560]{1,0:T(8,128)(2,1)}, bf16[256,2560]{1,0:T(8,128)(2,1)S(1)}, u32[]{:S(2)}, u32[]{:S(2)}) collective-permute-start(bf16[256,2560]{1,0:T(8,128)(2,1)} %get-tuple-element.265), channel_id=1, source_target_pairs={{0,16},{16,0},{1,17},{17,1},{2,18},{18,2},{3,19},{19,3},{4,20},{20... | collective-permute-start | bytes 3932168 | tf_op jit(solution)/shard_map/ppermute | solution.py:23
  273.2 34.7 %collective-permute-start.56 = (bf16[960,256]{1,0:T(8,128)(2,1)S(1)}, bf16[960,256]{1,0:T(8,128)(2,1)S(1)}, u32[]{:S(2)}, u32[]{:S(2)}) collective-permute-start(bf16[960,256]{1,0:T(8,128)(2,1)S(1)} %get-tuple-element.263.refs_0_), channel_id=1, source_target_pairs={{0,16},{16,0},{1,17},{17,1},{2,18},{18,2},{3,19},{19,3},{4,20},{20... | collective-permute-start | bytes 1474568 | tf_op jit(solution)/shard_map/ppermute | solution.py:23
  281.2 43.7 %collective-permute-start.60 = (bf16[2,640,512]{2,1,0:T(8,128)(2,1)}, bf16[2,640,512]{2,1,0:T(8,128)(2,1)}, u32[]{:S(2)}, u32[]{:S(2)}) collective-permute-start(bf16[2,640,512]{2,1,0:T(8,128)(2,1)} %get-tuple-element.250), channel_id=1, source_target_pairs={{0,4},{4,0},{8,12},{12,8},{16,24},{20,28},{24,16},{28,20},{1,5},{5... | collective-permute-start | bytes 3932168 | tf_op jit(solution)/shard_map/ppermute | solution.py:66
  305.4 16.4 %collective-permute-start.58 = (bf16[640,256]{1,0:T(8,128)(2,1)S(1)}, bf16[640,256]{1,0:T(8,128)(2,1)S(1)}, u32[]{:S(2)}, u32[]{:S(2)}) collective-permute-start(bf16[640,256]{1,0:T(8,128)(2,1)S(1)} %get-tuple-element.270), channel_id=1, source_target_pairs={{0,8},{4,12},{8,0},{12,4},{1,9},{5,13},{9,1},{13,5},{2,10},{6,14},... | collective-permute-start | bytes 983048 | tf_op jit(solution)/shard_map/ppermute | solution.py:32
  307.9 15.2 %collective-permute-start.59 = (bf16[640,256]{1,0:T(8,128)(2,1)S(1)}, bf16[640,256]{1,0:T(8,128)(2,1)S(1)}, u32[]{:S(2)}, u32[]{:S(2)}) collective-permute-start(bf16[640,256]{1,0:T(8,128)(2,1)S(1)} %get-tuple-element.272), channel_id=1, source_target_pairs={{0,12},{4,8},{8,4},{12,0},{1,13},{5,9},{9,5},{13,1},{2,14},{6,10},... | collective-permute-start | bytes 983048 | tf_op jit(solution)/shard_map/ppermute | solution.py:32
  323.8 49.1 %collective-permute-start.70 = (bf16[2,240,2560]{2,1,0:T(8,128)(2,1)}, bf16[2,240,2560]{2,1,0:T(8,128)(2,1)}, u32[]{:S(2)}, u32[]{:S(2)}) collective-permute-start(bf16[2,240,2560]{2,1,0:T(8,128)(2,1)} %get-tuple-element.306), channel_id=1, source_target_pairs={{0,4},{4,0},{8,12},{12,8},{16,24},{20,28},{24,16},{28,20},{1,5},{5... | collective-permute-start | bytes 7372808 | tf_op jit(solution)/shard_map/ppermute | solution.py:66
  324.9 13.3 %collective-permute-start.64 = (bf16[960,256]{1,0:T(8,128)(2,1)S(1)}, bf16[960,256]{1,0:T(8,128)(2,1)S(1)}, u32[]{:S(2)}, u32[]{:S(2)}) collective-permute-start(bf16[960,256]{1,0:T(8,128)(2,1)S(1)} %copy-done.29), channel_id=1, source_target_pairs={{0,16},{16,0},{1,17},{17,1},{2,18},{18,2},{3,19},{19,3},{4,20},{20... | collective-permute-start | bytes 1474568 | tf_op jit(solution)/shard_map/ppermute | solution.py:23
  327.3 20.9 %collective-permute-start.61 = (bf16[640,512]{1,0:T(8,128)(2,1)}, bf16[640,512]{1,0:T(8,128)(2,1)}, u32[]{:S(2)}, u32[]{:S(2)}) collective-permute-start(bf16[640,512]{1,0:T(8,128)(2,1)} %fusion.9), channel_id=1, source_target_pairs={{0,8},{4,12},{8,0},{12,4},{16,20},{20,16},{24,28},{28,24},{1,9},{5... | collective-permute-start | bytes 1966088 | tf_op jit(solution)/shard_map/ppermute | solution.py:71
  352.4 48.0 %collective-permute-start.69 = (bf16[2,240,1280]{2,1,0:T(8,128)(2,1)}, bf16[2,240,1280]{2,1,0:T(8,128)(2,1)}, u32[]{:S(2)}, u32[]{:S(2)}) collective-permute-start(bf16[2,240,1280]{2,1,0:T(8,128)(2,1)} %copy-done.109), channel_id=1, source_target_pairs={{0,4},{4,0},{8,12},{12,8},{16,24},{20,28},{24,16},{28,20},{1,5},{5... | collective-permute-start | bytes 3686408 | tf_op jit(solution)/shard_map/ppermute | solution.py:66
  353.3 120.6 %reduce-scatter.8.cloned.1.call-start = ((), (), s32[]{:S(2)}) async-start(), calls=%async_computation.6 | async-start | bytes 1638400 | tf_op jit(solution)/shard_map/reduce_scatter | solution.py:618
  358.1 44.4 %collective-permute-start.68 = (bf16[2,640,512]{2,1,0:T(8,128)(2,1)}, bf16[2,640,512]{2,1,0:T(8,128)(2,1)}, u32[]{:S(2)}, u32[]{:S(2)}) collective-permute-start(bf16[2,640,512]{2,1,0:T(8,128)(2,1)} %get-tuple-element.288), channel_id=1, source_target_pairs={{0,4},{4,0},{8,12},{12,8},{16,24},{20,28},{24,16},{28,20},{1,5},{5... | collective-permute-start | bytes 3932168 | tf_op jit(solution)/shard_map/ppermute | solution.py:66
  372.6 32.3 %collective-permute-start.67 = (bf16[256,2560]{1,0:T(8,128)(2,1)}, bf16[256,2560]{1,0:T(8,128)(2,1)}, u32[]{:S(2)}, u32[]{:S(2)}) collective-permute-start(bf16[256,2560]{1,0:T(8,128)(2,1)} %get-tuple-element.293), channel_id=1, source_target_pairs={{0,16},{16,0},{1,17},{17,1},{2,18},{18,2},{3,19},{19,3},{4,20},{20... | collective-permute-start | bytes 3932168 | tf_op jit(solution)/shard_map/ppermute | solution.py:23
  376.0 38.5 %collective-permute-start.74 = (bf16[240,2560]{1,0:T(8,128)(2,1)}, bf16[240,2560]{1,0:T(8,128)(2,1)}, u32[]{:S(2)}, u32[]{:S(2)}) collective-permute-start(bf16[240,2560]{1,0:T(8,128)(2,1)} %fusion.5), channel_id=1, source_target_pairs={{0,8},{4,12},{8,0},{12,4},{16,20},{20,16},{24,28},{28,24},{1,9},{5... | collective-permute-start | bytes 3686408 | tf_op jit(solution)/shard_map/ppermute | solution.py:71
  412.2 16.8 %collective-permute-start.72 = (bf16[640,256]{1,0:T(8,128)(2,1)}, bf16[640,256]{1,0:T(8,128)(2,1)}, u32[]{:S(2)}, u32[]{:S(2)}) collective-permute-start(bf16[640,256]{1,0:T(8,128)(2,1)} %get-tuple-element.321), channel_id=1, source_target_pairs={{0,8},{4,12},{8,0},{12,4},{1,9},{5,13},{9,1},{13,5},{2,10},{6,14},... | collective-permute-start | bytes 983048 | tf_op jit(solution)/shard_map/ppermute | solution.py:32
  413.0 16.0 %collective-permute-start.71 = (bf16[640,256]{1,0:T(8,128)(2,1)}, bf16[640,256]{1,0:T(8,128)(2,1)}, u32[]{:S(2)}, u32[]{:S(2)}) collective-permute-start(bf16[640,256]{1,0:T(8,128)(2,1)} %get-tuple-element.320), channel_id=1, source_target_pairs={{0,12},{4,8},{8,4},{12,0},{1,13},{5,9},{9,5},{13,1},{2,14},{6,10},... | collective-permute-start | bytes 983048 | tf_op jit(solution)/shard_map/ppermute | solution.py:32
  420.1 76.4 %reduce-scatter.10.cloned.1.call-start = ((), (), s32[]{:S(2)}) async-start(), calls=%async_computation.7 | async-start | bytes 819200 | tf_op jit(solution)/shard_map/reduce_scatter | solution.py:618
  429.0 45.0 %collective-permute-start.75 = (bf16[2,240,2560]{2,1,0:T(8,128)(2,1)}, bf16[2,240,2560]{2,1,0:T(8,128)(2,1)}, u32[]{:S(2)}, u32[]{:S(2)}) collective-permute-start(bf16[2,240,2560]{2,1,0:T(8,128)(2,1)} %copy-done.108), channel_id=1, source_target_pairs={{0,4},{4,0},{8,12},{12,8},{16,24},{20,28},{24,16},{28,20},{1,5},{5... | collective-permute-start | bytes 7372808 | tf_op jit(solution)/shard_map/ppermute | solution.py:66
  440.6 16.8 %collective-permute-start.77 = (bf16[240,1280]{1,0:T(8,128)(2,1)S(1)}, bf16[240,1280]{1,0:T(8,128)(2,1)S(1)}, u32[]{:S(2)}, u32[]{:S(2)}) collective-permute-start(bf16[240,1280]{1,0:T(8,128)(2,1)S(1)} %copy-done.121), channel_id=1, source_target_pairs={{0,8},{4,12},{8,0},{12,4},{16,20},{20,16},{24,28},{28,24},{1,9},{5... | collective-permute-start | bytes 1843208 | tf_op jit(solution)/shard_map/ppermute | solution.py:71
  442.2 29.4 %collective-permute-start.76 = (bf16[640,512]{1,0:T(8,128)(2,1)}, bf16[640,512]{1,0:T(8,128)(2,1)}, u32[]{:S(2)}, u32[]{:S(2)}) collective-permute-start(bf16[640,512]{1,0:T(8,128)(2,1)} %fusion.10), channel_id=1, source_target_pairs={{0,8},{4,12},{8,0},{12,4},{16,20},{20,16},{24,28},{28,24},{1,9},{5... | collective-permute-start | bytes 1966088 | tf_op jit(solution)/shard_map/ppermute | solution.py:71
  443.7 34.9 %collective-permute-start.52 = (bf16[256,960]{1,0:T(8,128)(2,1)}, bf16[256,960]{1,0:T(8,128)(2,1)}, u32[]{:S(2)}, u32[]{:S(2)}) collective-permute-start(bf16[256,960]{1,0:T(8,128)(2,1)} %broadcast_select_fusion.2), channel_id=1, source_target_pairs={{0,16},{16,0},{1,17},{17,1},{2,18},{18,2},{3,19},{19,3},{4,20},{20... | collective-permute-start | bytes 1474568 | tf_op jit(solution)/shard_map/ppermute | solution.py:23
  449.2 45.2 %collective-permute-start.85 = (bf16[2,256,1280]{2,1,0:T(8,128)(2,1)}, bf16[2,256,1280]{2,1,0:T(8,128)(2,1)}, u32[]{:S(2)}, u32[]{:S(2)}) collective-permute-start(bf16[2,256,1280]{2,1,0:T(8,128)(2,1)} %get-tuple-element.342), channel_id=1, source_target_pairs={{0,4},{4,0},{8,12},{12,8},{16,24},{20,28},{24,16},{28,20},{1,5},{5... | collective-permute-start | bytes 3932168 | tf_op jit(solution)/shard_map/ppermute | solution.py:66
  461.7 72.8 %reduce-scatter.12.cloned.1.call-start = ((), (), s32[]{:S(2)}) async-start(), calls=%async_computation.8 | async-start | bytes 819200 | tf_op jit(solution)/shard_map/reduce_scatter | solution.py:618
  477.0 20.5 %collective-permute-start.84 = (bf16[240,2560]{1,0:T(8,128)(2,1)}, bf16[240,2560]{1,0:T(8,128)(2,1)}, u32[]{:S(2)}, u32[]{:S(2)}) collective-permute-start(bf16[240,2560]{1,0:T(8,128)(2,1)} %fusion.6), channel_id=1, source_target_pairs={{0,8},{4,12},{8,0},{12,4},{16,20},{20,16},{24,28},{28,24},{1,9},{5... | collective-permute-start | bytes 3686408 | tf_op jit(solution)/shard_map/ppermute | solution.py:71
  480.8 81.1 %reduce-scatter.14.cloned.1.call-start = ((), (), s32[]{:S(2)}) async-start(), calls=%async_computation.9 | async-start | bytes 1638400 | tf_op jit(solution)/shard_map/reduce_scatter | solution.py:618
  508.2 26.1 %collective-permute-start.87 = (bf16[2,76,1280]{2,1,0:T(8,128)(2,1)S(1)}, bf16[2,76,1280]{2,1,0:T(8,128)(2,1)S(1)}, u32[]{:S(2)}, u32[]{:S(2)}) collective-permute-start(bf16[2,76,1280]{2,1,0:T(8,128)(2,1)S(1)} %fusion.15), channel_id=1, source_target_pairs={{0,1},{1,0},{2,3},{3,2},{4,5},{5,4},{6,7},{7,6},{8,9},{9,8},{10,11... | collective-permute-start | bytes 1167368 | tf_op jit(solution)/shard_map/ppermute | solution.py:32
  537.3 22.8 %collective-permute-start.88 = (bf16[76,1280]{1,0:T(8,128)(2,1)S(1)}, bf16[76,1280]{1,0:T(8,128)(2,1)S(1)}, u32[]{:S(2)}, u32[]{:S(2)}) collective-permute-start(bf16[76,1280]{1,0:T(8,128)(2,1)S(1)} %dynamic-slice_bitcast_fusion.1), channel_id=1, source_target_pairs={{0,2},{1,3},{2,0},{3,1},{4,6},{5,7},{6,4},{7,5},{8,10},{9,11},{10,... | collective-permute-start | bytes 583688 | tf_op jit(solution)/shard_map/ppermute | solution.py:32
  (166 other events, 858.6 us)
Sparse Core Ops, SparseCore 0:
  13.5 45.5 all-gather.6
  77.2 45.8 all-gather.8
  150.3 41.5 all-gather.10
  353.5 31.6 reduce-scatter.5
  420.2 40.5 reduce-scatter.7
  463.6 29.3 reduce-scatter.9
  495.8 21.0 reduce-scatter.11
  519.9 37.7 reduce-scatter.13
